TPU v7x, 256 devices: a whole 4x4x8 slice. The times are simulated.
256 devices in a mesh: fsdp: 32 (over z, y), tensor: 8 (over x, core).
Axes of the slice: x: 4, y: 4, z: 8, core: 2. Of those that a mesh axis runs over, the one named last changes fastest.
Arguments:
- momentum: float32 [16384, 9216], P('fsdp', 'tensor'), may hold values from -6 to 6
- gradient: bfloat16 [16384, 9216], P('fsdp', 'tensor'), may hold values from -3 to 3
- weights: float32 [16384, 9216], P('fsdp', 'tensor'), may hold values from -6 to 6
- prior_right: float32 [9216, 256], P('tensor'), may hold values from -6 to 6
Outputs:
- new_momentum: float32 [16384, 9216], P('fsdp', 'tensor')
- new_weights: float32 [16384, 9216], P('fsdp', 'tensor')
- new_right: float32 [9216, 256], P('tensor')
All inputs are finite; a program needn't handle non-finite values.
Results may differ from a plain program's by a relative error of at most 0.0003.
Values sent between devices are 32-bit elements; how exact they have to be, the bound alone decides.
A program may use at most 64 MiB of HBM per device.

v0:
```python
import math

import jax
import jax.numpy as jnp
from jax import lax
from jax.sharding import PartitionSpec as P

ROWS = 16384
COLS = 9216
RANK = 256


def partner_2(block, axis, stride):
    count = lax.axis_size(axis)
    route = []
    for low in range(count):
        high = low | 1 << stride
        if high != low and high < count:
            route += [(low, high), (high, low)]
    return lax.ppermute(block, axis, route)


def matmul_high(left_mat, right_mat):
    return jnp.dot(
        left_mat, right_mat, precision=lax.Precision.HIGHEST, preferred_element_type=jnp.float32
    )


def contract_rows(left_mat, right_mat):
    return lax.dot_general(
        left_mat,
        right_mat,
        (((0,), (0,)), ((), ())),
        precision=lax.Precision.HIGHEST,
        preferred_element_type=jnp.float32,
    )


def body(momentum, gradient, weights, prior_right):
    buffer = momentum + gradient.astype(jnp.float32)
    projected = lax.psum(matmul_high(buffer, prior_right), "tensor")
    factor = jnp.linalg.cholesky(contract_rows(projected, projected))
    for bit_level in range(lax.axis_size("fsdp").bit_length() - 1):
        partner = partner_2(factor, "fsdp", bit_level)
        summed = matmul_high(factor, factor.T) + matmul_high(partner, partner.T)
        factor = jnp.linalg.cholesky(summed)
    ortho_basis = lax.linalg.triangular_solve(
        factor, projected, left_side=False, lower=True, transpose_a=True
    )
    right_factor = lax.psum(contract_rows(buffer, ortho_basis), "fsdp")
    totals = lax.psum(jnp.sum(right_factor * right_factor, axis=0), "tensor")
    col_scale = lax.rsqrt(totals / COLS + 1e-06)
    new_right = right_factor * col_scale[None, :]
    new_momentum = buffer - 0.5 * matmul_high(ortho_basis, right_factor.T)
    step_size = 0.2 * math.sqrt(ROWS / RANK)
    new_weights = weights - step_size * matmul_high(ortho_basis, new_right.T)
    return (new_momentum, new_weights, new_right)


def solution(mesh):
    in_specs = (P("fsdp", "tensor"), P("fsdp", "tensor"), P("fsdp", "tensor"), P("tensor", None))
    out_specs = (P("fsdp", "tensor"), P("fsdp", "tensor"), P("tensor", None))
    return jax.shard_map(body, mesh=mesh, in_specs=in_specs, out_specs=out_specs, check_vma=False)
```

profile of v0, /device:TPU:1, one launch (start us, length us, event | category | flops | bytes accessed | tf_op | source)
XLA Modules:
  0.0 600.8 jit_solution(1794306823440412168)
XLA Ops:
  8.4 5.0 fusion.3
  13.7 67.4 %all-reduce.4.cloned.1.call-done = f32[512,256]{1,0:T(8,128)} async-done(((f32[512,256]{1,0:T(8,128)}), f32[512,256]{1,0:T(8,128)}) %all-reduce.4.cloned.1.call-update) | async-done | bytes 524304 | tf_op jit(solution)/shard_map/psum | solution.py:41
  83.6 11.7 %cholesky.298 = f32[128,128]{1,0:T(8,128)S(1)} custom-call(f32[128,128]{1,0:T(8,128)S(1)} %cholesky.498), custom_call_target="Cholesky" | custom-call | tf_op jit(solution)/shard_map/jit(cholesky)/cholesky | solution.py:42
  95.3 9.8 %custom-call.17 = f32[1,128,128]{1,2,0:T(8,128)S(1)} custom-call(f32[1,128,128]{2,1,0:T(8,128)S(1)} %get-tuple-element.45), custom_call_target="InvertDiagBlocksLowerTriangular" | custom-call | tf_op jit(solution)/shard_map/jit(cholesky)/cholesky | solution.py:42
  105.6 11.7 %cholesky.315 = f32[128,128]{1,0:T(8,128)S(1)} custom-call(f32[128,128]{1,0:T(8,128)S(1)} %convolution_subtract_fusion.1), custom_call_target="Cholesky" | custom-call | tf_op jit(solution)/shard_map/jit(cholesky)/cholesky | solution.py:42
  121.3 3.6 collective-permute-done
  125.5 11.7 %cholesky.332 = f32[128,128]{1,0:T(8,128)S(1)} custom-call(f32[128,128]{1,0:T(8,128)S(1)} %cholesky.501), custom_call_target="Cholesky" | custom-call | tf_op jit(solution)/shard_map/jit(cholesky)/cholesky | solution.py:46
  137.9 9.8 %custom-call.18 = f32[1,128,128]{1,2,0:T(8,128)S(1)} custom-call(f32[1,128,128]{2,1,0:T(8,128)S(1)} %get-tuple-element.41), custom_call_target="InvertDiagBlocksLowerTriangular" | custom-call | tf_op jit(solution)/shard_map/jit(cholesky)/cholesky | solution.py:46
  148.2 11.7 %cholesky.349 = f32[128,128]{1,0:T(8,128)S(1)} custom-call(f32[128,128]{1,0:T(8,128)S(1)} %slice_subtract_fusion.4), custom_call_target="Cholesky" | custom-call | tf_op jit(solution)/shard_map/jit(cholesky)/cholesky | solution.py:46
  165.6 3.6 collective-permute-done.1
  169.8 11.7 %cholesky.366 = f32[128,128]{1,0:T(8,128)S(1)} custom-call(f32[128,128]{1,0:T(8,128)S(1)} %cholesky.504), custom_call_target="Cholesky" | custom-call | tf_op jit(solution)/shard_map/jit(cholesky)/cholesky | solution.py:46
  182.2 9.8 %custom-call.19 = f32[1,128,128]{1,2,0:T(8,128)S(1)} custom-call(f32[1,128,128]{2,1,0:T(8,128)S(1)} %get-tuple-element.37), custom_call_target="InvertDiagBlocksLowerTriangular" | custom-call | tf_op jit(solution)/shard_map/jit(cholesky)/cholesky | solution.py:46
  192.5 11.7 %cholesky.383 = f32[128,128]{1,0:T(8,128)S(1)} custom-call(f32[128,128]{1,0:T(8,128)S(1)} %slice_subtract_fusion.3), custom_call_target="Cholesky" | custom-call | tf_op jit(solution)/shard_map/jit(cholesky)/cholesky | solution.py:46
  212.3 11.7 %cholesky.400 = f32[128,128]{1,0:T(8,128)S(1)} custom-call(f32[128,128]{1,0:T(8,128)S(1)} %cholesky.507), custom_call_target="Cholesky" | custom-call | tf_op jit(solution)/shard_map/jit(cholesky)/cholesky | solution.py:46
  224.7 9.8 %custom-call.20 = f32[1,128,128]{1,2,0:T(8,128)S(1)} custom-call(f32[1,128,128]{2,1,0:T(8,128)S(1)} %get-tuple-element.33), custom_call_target="InvertDiagBlocksLowerTriangular" | custom-call | tf_op jit(solution)/shard_map/jit(cholesky)/cholesky | solution.py:46
  235.0 11.7 %cholesky.417 = f32[128,128]{1,0:T(8,128)S(1)} custom-call(f32[128,128]{1,0:T(8,128)S(1)} %slice_subtract_fusion.2), custom_call_target="Cholesky" | custom-call | tf_op jit(solution)/shard_map/jit(cholesky)/cholesky | solution.py:46
  251.7 6.2 %collective-permute-done.3 = f32[256,256]{1,0:T(8,128)S(1)} collective-permute-done((f32[256,256]{1,0:T(8,128)S(1)}, f32[256,256]{1,0:T(8,128)S(1)}, u32[]{:S(2)}, u32[]{:S(2)}) %collective-permute-start.3) | collective-permute-done | bytes 262176 | tf_op jit(solution)/shard_map/ppermute | solution.py:20
  258.6 11.7 %cholesky.434 = f32[128,128]{1,0:T(8,128)S(1)} custom-call(f32[128,128]{1,0:T(8,128)S(1)} %cholesky.510), custom_call_target="Cholesky" | custom-call | tf_op jit(solution)/shard_map/jit(cholesky)/cholesky | solution.py:46
  271.0 9.8 %custom-call.21 = f32[1,128,128]{1,2,0:T(8,128)S(1)} custom-call(f32[1,128,128]{2,1,0:T(8,128)S(1)} %get-tuple-element.29), custom_call_target="InvertDiagBlocksLowerTriangular" | custom-call | tf_op jit(solution)/shard_map/jit(cholesky)/cholesky | solution.py:46
  281.3 11.7 %cholesky.451 = f32[128,128]{1,0:T(8,128)S(1)} custom-call(f32[128,128]{1,0:T(8,128)S(1)} %slice_subtract_fusion.1), custom_call_target="Cholesky" | custom-call | tf_op jit(solution)/shard_map/jit(cholesky)/cholesky | solution.py:46
  295.0 5.9 collective-permute-start.4
  301.4 6.1 %collective-permute-done.4 = f32[256,256]{1,0:T(8,128)S(1)} collective-permute-done((f32[256,256]{1,0:T(8,128)S(1)}, f32[256,256]{1,0:T(8,128)S(1)}, u32[]{:S(2)}, u32[]{:S(2)}) %collective-permute-start.4) | collective-permute-done | bytes 262176 | tf_op jit(solution)/shard_map/ppermute | solution.py:20
  309.4 13.3 %cholesky.468 = f32[128,128]{1,0:T(8,128)} custom-call(f32[128,128]{1,0:T(8,128)} %cholesky.513), custom_call_target="Cholesky" | custom-call | tf_op jit(solution)/shard_map/jit(cholesky)/cholesky | solution.py:46
  326.4 11.3 %custom-call.22 = f32[1,128,128]{1,2,0:T(8,128)} custom-call(f32[1,128,128]{2,1,0:T(8,128)} %get-tuple-element.25), custom_call_target="InvertDiagBlocksLowerTriangular" | custom-call | tf_op jit(solution)/shard_map/jit(cholesky)/cholesky | solution.py:46
  341.1 13.2 %cholesky.485 = f32[128,128]{1,0:T(8,128)} custom-call(f32[128,128]{1,0:T(8,128)} %slice_subtract_fusion), custom_call_target="Cholesky" | custom-call | tf_op jit(solution)/shard_map/jit(cholesky)/cholesky | solution.py:46
  359.4 7.2 %while.1 = (s32[]{:T(128)}, f32[256,256]{1,0:T(8,128)}, s32[2,2]{1,0:T(2,128)S(1)}, f32[2,128,128]{2,1,0:T(8,128)}, s32[]{:T(128)}) while((s32[]{:T(128)}, f32[256,256]{1,0:T(8,128)}, s32[2,2]{1,0:T(2,128)S(1)}, f32[2,128,128]{2,1,0:T(8,128)}, s32[]{:T(128)}) %tuple.43), condition=%wide.while_cond, body=%wide.while_body.sunk | while | flops 2 | bytes 132205 | solution.py:47
  366.7 21.1 %custom-call.11 = f32[2,128,128]{1,2,0:T(8,128)} custom-call(f32[2,128,128]{2,1,0:T(8,128)} %get-tuple-element.11), custom_call_target="InvertDiagBlocksLowerTriangular" | custom-call | tf_op jit(solution)/shard_map/triangular_solve | solution.py:47
  392.9 4.9 fusion.2
  397.9 161.8 %all-reduce.6.cloned.1.call-done = f32[1152,256]{1,0:T(8,128)} async-done(((f32[1152,256]{1,0:T(8,128)}), f32[1152,256]{1,0:T(8,128)}) %all-reduce.6.cloned.1.call-update) | async-done | bytes 1179664 | tf_op jit(solution)/shard_map/psum | solution.py:50
  561.1 17.3 %psum.23 = f32[256]{0:T(256)S(1)} all-reduce(f32[256]{0:T(256)S(1)} %multiply_reduce_fusion), channel_id=1, replica_groups=mesh['fsdp'=32,'tensor'=8] {'tensor'}, use_global_device_ids=true, to_apply=%region_7.9 | all-reduce | flops 256 | bytes 2048 | tf_op jit(solution)/shard_map/psum | solution.py:51
  579.9 7.9 %fusion.1 = f32[512,1152]{1,0:T(8,128)} fusion(f32[512,1152]{1,0:T(8,128)} %param.7, f32[1152,256]{1,0:T(8,128)S(1)} %broadcast_multiply_fusion, f32[512,128]{0,1:T(8,128)S(1)} %copy-done.9, f32[512,128]{0,1:T(8,128)S(1)} %copy-done.6), kind=kOutput, calls=%fused_computation.5 | convolution fusion | flops 1813250048 | bytes 6422528 | tf_op jit(solution)/shard_map/dot_general | solution.py:24
  587.8 5.9 fusion
  (122 shorter events, 57.3 us)
Async XLA Ops:
  7.2 1.3 copy-start
  7.2 74.0 %all-reduce.4.cloned.1.call-start = ((), (), s32[]{:S(2)}) async-start(), calls=%async_computation | async-start | bytes 1048576 | tf_op jit(solution)/shard_map/psum | solution.py:41
  13.5 546.2 %all-reduce.6.cloned.1.call-start = ((), (), s32[]{:S(2)}) async-start(), calls=%async_computation.1 | async-start | bytes 2359296 | tf_op jit(solution)/shard_map/psum | solution.py:50
  119.4 5.5 collective-permute-start
  161.9 7.2 %collective-permute-start.1 = (f32[256,256]{1,0:T(8,128)S(1)}, f32[256,256]{1,0:T(8,128)S(1)}, u32[]{:S(2)}, u32[]{:S(2)}) collective-permute-start(f32[256,256]{1,0:T(8,128)S(1)} %select_select_fusion.4), channel_id=1, source_target_pairs={{0,16},{16,0},{8,24},{24,8},{32,48},{48,32},{40,56},{56,40},{64,80... | collective-permute-start | bytes 786440 | tf_op jit(solution)/shard_map/ppermute | solution.py:20
  206.2 5.5 collective-permute-start.2
  248.7 9.2 %collective-permute-start.3 = (f32[256,256]{1,0:T(8,128)S(1)}, f32[256,256]{1,0:T(8,128)S(1)}, u32[]{:S(2)}, u32[]{:S(2)}) collective-permute-start(f32[256,256]{1,0:T(8,128)S(1)} %select_select_fusion.2), channel_id=1, source_target_pairs={{0,64},{64,0},{8,72},{72,8},{16,80},{80,16},{24,88},{88,24},{32,96... | collective-permute-start | bytes 786440 | tf_op jit(solution)/shard_map/ppermute | solution.py:20
  295.0 12.5 %collective-permute-start.4 = (f32[256,256]{1,0:T(8,128)S(1)}, f32[256,256]{1,0:T(8,128)S(1)}, u32[]{:S(2)}, u32[]{:S(2)}) collective-permute-start(f32[256,256]{1,0:T(8,128)S(1)} %select_select_fusion.1), channel_id=1, source_target_pairs={{0,128},{128,0},{8,136},{136,8},{16,144},{144,16},{24,152},{152,24... | collective-permute-start | bytes 786440 | tf_op jit(solution)/shard_map/ppermute | solution.py:20
  308.1 0.7 copy-start.10
  308.8 84.2 %copy-start.1 = (f32[512,1152]{1,0:T(8,128)S(1)}, f32[512,1152]{1,0:T(8,128)}, u32[]{:S(2)}) copy-start(f32[512,1152]{1,0:T(8,128)} %param.5) | copy-start | bytes 7077892
  387.8 5.2 copy-start.2
  389.3 3.0 copy-start.5
  392.2 0.7 copy-start.8
  578.4 1.4 copy-start.6
  578.4 1.4 copy-start.9
  579.9 8.0 %copy-start.7 = (f32[1152,256]{1,0:T(8,128)}, f32[1152,256]{1,0:T(8,128)S(1)}, u32[]{:S(2)}) copy-start(f32[1152,256]{1,0:T(8,128)S(1)} %broadcast_multiply_fusion) | copy-start | bytes 3538948
  579.9 8.0 %copy-start.3 = (bf16[512,1152]{1,0:T(8,128)(2,1)S(1)}, bf16[512,1152]{1,0:T(8,128)(2,1)}, u32[]{:S(2)}) copy-start(bf16[512,1152]{1,0:T(8,128)(2,1)} %param.6) | copy-start | bytes 3538948
  579.9 8.0 %copy-start.4 = (f32[1152,256]{1,0:T(8,128)S(1)}, f32[1152,256]{1,0:T(8,128)}, u32[]{:S(2)}) copy-start(f32[1152,256]{1,0:T(8,128)} %all-reduce.6.cloned.1.call-done) | copy-start | bytes 3538948
Sparse Core Ops, SparseCore 0:
  13.6 67.4 all-reduce.3
  398.0 161.6 all-reduce.5
where the time goes:
time: 604 us; the launch traced here: 601 us
  waiting for transfers between devices  252 us (42%)
  other arithmetic  240 us (40%)
  matrix products  40.3 us (7%)
  between operations  22.6 us (4%)
  blocking collectives  17.3 us (3%)
  starting transfers between devices  15 us (2%)
  local copies, waits for them, and re-layouts  12.9 us (2%)
    another operation x35, other arithmetic, body(): factor = jnp.linalg.cholesky(summed)  180 us
    psum x1, waiting for transfers between devices, body(): right_factor = lax.psum(contract_rows(buffer, ortho_basis), 'fsdp')  162 us
    psum x1, waiting for transfers between devices, body(): projected = lax.psum(matmul_high(buffer, prior_right), 'tensor')  67.4 us
    another operation x6, other arithmetic, body(): factor = jnp.linalg.cholesky(contract_rows(projected, projected))  34 us
    ppermute x5, waiting for transfers between devices, partner_2(): return lax.ppermute(block, axis, route)  23.1 us
    dot_general x13, matrix products, matmul_high(): jnp.dot(left_mat, right_mat, precision=lax.Precision.HIGHEST, preferred_e...  23 us
    another operation x3, other arithmetic, body(): lax.linalg.triangular_solve(factor, projected, left_side=False, lower=Tru...  22.8 us
    psum x1, blocking collectives, body(): totals = lax.psum(jnp.sum(right_factor * right_factor, axis=0), 'tensor')  17.3 us
  transfers between devices with their start and end apart: 7, of which 7 were waited for; matrix products, arithmetic and copies ran while one was open for 0% of the time, Pallas kernels for 0%

commit v1 on v0

v1 whole, which is shorter than its diff:
```python
import functools
import math

import jax
import jax.numpy as jnp
from jax import lax
from jax.experimental import pallas as pl
from jax.experimental.pallas import tpu as pltpu
from jax.sharding import PartitionSpec as P

ROWS = 16384
COLS = 9216
RANK = 256
NZ, NY, NX = 8, 4, 4
BR = 512
BC = 1152
HALF = 128
LEAF = 64
PANEL = 16
F32 = jnp.float32
BF16 = jnp.bfloat16
MESH = pl.DeviceIdType.MESH
CHUNKS = ((0, 256, "z"), (256, 512, "y"), (768, 384, "y"))


def dot_f32(a, b, ca, cb):
    return lax.dot_general(
        a, b, (((ca,), (cb,)), ((), ())), precision=lax.Precision.HIGHEST, preferred_element_type=F32
    )


def split(a):
    hi = a.astype(BF16)
    return hi, (a - hi.astype(F32)).astype(BF16)


def dot_bf16(a, b, ca, cb):
    return lax.dot_general(a, b, (((ca,), (cb,)), ((), ())), preferred_element_type=F32)


def dot3(a, b, ca, cb):
    return dot_bf16(a[0], b[0], ca, cb) + (dot_bf16(a[0], b[1], ca, cb) + dot_bf16(a[1], b[0], ca, cb))


def leaf_elimination(block):
    n = block.shape[0]
    row = lax.broadcasted_iota(jnp.int32, (n, n), 0)
    lane = lax.broadcasted_iota(jnp.int32, (n, n), 1)
    for p0 in range(0, n, PANEL):
        cols = [jnp.broadcast_to(block[p0:, p0 + j : p0 + j + 1], (n - p0, n)) for j in range(PANEL)]
        rw, ln, low = row[p0:], lane[p0:], block[p0:]
        for k in range(PANEL):
            r = 1.0 / cols[k][k : k + 1, :]
            f = jnp.where(rw > p0 + k, cols[k] * r, 0.0)
            for j in range(k + 1, PANEL):
                cols[j] = cols[j] - f * cols[j][k : k + 1, :]
            pivot_row = jnp.where(ln[0:1] == p0 + k, 1.0, low[k : k + 1, :])
            cleared = jnp.where((ln == p0 + k) & (rw > p0 + k), 0.0, low)
            low = cleared - f * pivot_row
        block = jnp.concatenate([block[:p0], low], axis=0) if p0 else low
    return block


def cholesky_inverse(a, between):
    blocks = RANK // LEAF
    for j in range(blocks):
        s = slice(j * LEAF, (j + 1) * LEAF)
        d = leaf_elimination(a[s, s])
        row = lax.broadcasted_iota(jnp.int32, (LEAF, LEAF), 0)
        lane = lax.broadcasted_iota(jnp.int32, (LEAF, LEAF), 1)
        pivot = jnp.sum(jnp.where(row == lane, d, 0.0), axis=1, keepdims=True)
        unit = jnp.where(row > lane, d, jnp.where(row == lane, 1.0, 0.0))
        inv = unit * lax.rsqrt(pivot)
        x = dot_f32(inv, a[s, :], 1, 0)
        a[s, :] = x
        a[s, s] = inv
        if j < blocks - 1:
            low = (j + 1) * LEAF
            a[low:, s] = jnp.zeros((RANK - low, LEAF), F32)
            a[low:, :] = a[low:, :] - dot_f32(x[:, low:], a[s, :], 0, 0)
            between(j)


def factor_kernel(
    m_ref, g_ref, v_ref, q_ref, rt_ref, norm_ref,
    bh, bl, part, crecv, half, xrecv, own, pfull, pt,
    gpart, gyrecv, gz, gmat,
    w, wf, r1y, r1z, s1y, s1z, r2y, r2z, s2,
    nbuf, c_s, c_r, x_s, x_r, g_s, g_r, w_s, w_r, n_s, n_r,
):
    fi, ti = lax.axis_index("fsdp"), lax.axis_index("tensor")
    z, y = fi // NY, lax.rem(fi, NY)
    x, c = ti // 2, lax.rem(ti, 2)

    def dev(zz, yy, xx, cc):
        return (zz * NY + yy, xx * 2 + cc)

    def peer_z(i):
        return lax.rem(z + i, NZ)

    def peer_y(i):
        return lax.rem(y + i, NY)

    def peer_x(i):
        return lax.rem(x + i, NX)

    pending = []

    def send(src, dst, ss, rs, to):
        copy = pltpu.make_async_remote_copy(
            src_ref=src, dst_ref=dst, send_sem=ss, recv_sem=rs, device_id=to, device_id_type=MESH
        )
        copy.start()
        pending.append(copy)
        return copy

    barrier = pltpu.get_barrier_semaphore()
    peers = [dev(z, peer_y(i), x, c) for i in range(1, NY)]
    peers += [dev(peer_z(i), y, x, c) for i in range(1, NZ)]
    tensor_peers = [dev(z, y, x, 1 - c)]
    tensor_peers += [dev(z, y, peer_x(i), cc) for i in range(1, NX) for cc in (c, 1 - c)]
    for p in peers + tensor_peers:
        pl.semaphore_signal(barrier, inc=1, device_id=p, device_id_type=MESH)

    buf = m_ref[...] + g_ref[...].astype(F32)
    bh[...], bl[...] = split(buf)

    def ds(start, size):
        return pl.ds(pl.multiple_of(start, 8), size)

    core_rs, x_rs, x_ag, core_ag = [], [], [], []
    for h in range(2):
        vh = split(v_ref[:, h * HALF : (h + 1) * HALF])
        part[h] = dot3((bh[...], bl[...]), vh, 1, 0)
        if h == 0:
            pl.semaphore_wait(barrier, len(peers + tensor_peers))
        core_rs.append(
            send(part.at[h, ds(256 * (1 - c), 256)], crecv.at[h], c_s.at[h, 0], c_r.at[h, 0], dev(z, y, x, 1 - c))
        )
    for h in range(2):
        core_rs[h].wait_recv()
        half[h] = part[h, ds(256 * c, 256), :] + crecv[h]
        x_rs.append([
            send(half.at[h, ds(64 * peer_x(i), 64)], xrecv.at[h, i - 1], x_s.at[h, 0, i - 1], x_r.at[h, 0, i - 1],
                 dev(z, y, peer_x(i), c))
            for i in range(1, NX)
        ])
    for h in range(2):
        for cp in x_rs[h]:
            cp.wait_recv()
        total = half[h, ds(64 * x, 64), :]
        for i in range(NX - 1):
            total = total + xrecv[h, i]
        own[h] = total
        at = 256 * c + 64 * x
        x_ag.append([
            send(own.at[h], pfull.at[h, ds(at, 64)], x_s.at[h, 1, i - 1], x_r.at[h, 1, i - 1], dev(z, y, peer_x(i), c))
            for i in range(1, NX)
        ])
        core_ag.append([
            send(own.at[h], pfull.at[h, ds(at, 64)], c_s.at[h, 1], c_r.at[h, 1], dev(z, y, x, 1 - c))
        ])
        pfull[h, ds(at, 64), :] = total
    for h in range(2):
        for i in range(1, NX):
            x_ag[h][i - 1].wait_recv()
            at = 256 * c + 64 * lax.rem(x + NX - i, NX)
            core_ag[h].append(
                send(pfull.at[h, ds(at, 64)], pfull.at[h, ds(at, 64)], c_s.at[h, 1 + i], c_r.at[h, 1 + i],
                     dev(z, y, x, 1 - c))
            )
        for cp in core_ag[h]:
            cp.wait_recv()
        ph = pfull[h].T
        pt[h * HALF : (h + 1) * HALF, :] = ph
        w[h * HALF : (h + 1) * HALF, :] = dot3(split(ph), (bh[...], bl[...]), 1, 0)

    rows = ds(32 * ti, 32)
    ptr = pt[rows, :]
    for h in range(2):
        gpart[:, h * HALF : (h + 1) * HALF] = dot_f32(ptr, pfull[h], 1, 0)
    g1 = [
        send(gpart.at[ds(8 * peer_y(i), 8)], gyrecv.at[i - 1], g_s.at[0, i - 1], g_r.at[0, i - 1],
             dev(z, peer_y(i), x, c))
        for i in range(1, NY)
    ]

    def to_y(i):
        return dev(z, peer_y(i), x, c)

    def to_z(i):
        return dev(peer_z(i), y, x, c)

    rs1, rs2, ag1, ag2 = {}, {}, {}, {}

    def start_rs1(n):
        c0, nc, first = CHUNKS[n]
        cs = pl.ds(c0, nc)
        if first == "y":
            rs1[n] = [
                send(w.at[ds(64 * peer_y(i), 64), cs], r1y.at[i - 1, :, cs], w_s.at[n, 0, i - 1], w_r.at[n, 0, i - 1], to_y(i))
                for i in range(1, NY)
            ]
        else:
            rs1[n] = [
                send(w.at[ds(32 * peer_z(i), 32), cs], r1z.at[i - 1, :, cs], w_s.at[n, 0, i - 1], w_r.at[n, 0, i - 1], to_z(i))
                for i in range(1, NZ)
            ]

    def start_rs2(n):
        c0, nc, first = CHUNKS[n]
        cs = pl.ds(c0, nc)
        for cp in rs1[n]:
            cp.wait_recv()
        if first == "y":
            total = w[ds(64 * y, 64), cs]
            for i in range(NY - 1):
                total = total + r1y[i, :, cs]
            s1y[:, cs] = total
            rs2[n] = [
                send(s1y.at[ds(8 * peer_z(i), 8), cs], r2z.at[i - 1, :, cs], w_s.at[n, 1, i - 1], w_r.at[n, 1, i - 1], to_z(i))
                for i in range(1, NZ)
            ]
        else:
            total = w[ds(32 * z, 32), cs]
            for i in range(NZ - 1):
                total = total + r1z[i, :, cs]
            s1z[:, cs] = total
            rs2[n] = [
                send(s1z.at[ds(8 * peer_y(i), 8), cs], r2y.at[i - 1, :, cs], w_s.at[n, 1, i - 1], w_r.at[n, 1, i - 1], to_y(i))
                for i in range(1, NY)
            ]

    def start_ag1(n):
        c0, nc, first = CHUNKS[n]
        cs = pl.ds(c0, nc)
        for cp in rs2[n]:
            cp.wait_recv()
        if first == "y":
            total = s1y[ds(8 * z, 8), cs]
            for i in range(NZ - 1):
                total = total + r2z[i, :, cs]
            at = 64 * y + 8 * z
            s2[:, cs] = total
            ag1[n] = [
                send(s2.at[:, cs], wf.at[ds(at, 8), cs], w_s.at[n, 2, i - 1], w_r.at[n, 2, i - 1], to_z(i))
                for i in range(1, NZ)
            ]
        else:
            total = s1z[ds(8 * y, 8), cs]
            for i in range(NY - 1):
                total = total + r2y[i, :, cs]
            at = 32 * z + 8 * y
            s2[:, cs] = total
            ag1[n] = [
                send(s2.at[:, cs], wf.at[ds(at, 8), cs], w_s.at[n, 2, i - 1], w_r.at[n, 2, i - 1], to_y(i))
                for i in range(1, NY)
            ]
        wf[ds(at, 8), cs] = total

    def start_ag2(n):
        c0, nc, first = CHUNKS[n]
        cs = pl.ds(c0, nc)
        for cp in ag1[n]:
            cp.wait_recv()
        if first == "y":
            piece = wf.at[ds(64 * y, 64), cs]
            ag2[n] = [
                send(piece, piece, w_s.at[n, 3, i - 1], w_r.at[n, 3, i - 1], to_y(i)) for i in range(1, NY)
            ]
        else:
            piece = wf.at[ds(32 * z, 32), cs]
            ag2[n] = [
                send(piece, piece, w_s.at[n, 3, i - 1], w_r.at[n, 3, i - 1], to_z(i)) for i in range(1, NZ)
            ]

    order = range(len(CHUNKS))
    for n in order:
        start_rs1(n)

    for cp in g1:
        cp.wait_recv()
    total = gpart[ds(8 * y, 8), :]
    for i in range(NY - 1):
        total = total + gyrecv[i]
    gz[z] = total
    g2 = [send(gz.at[z], gz.at[z], g_s.at[1, i - 1], g_r.at[1, i - 1], to_z(i)) for i in range(1, NZ)]
    for cp in g2:
        cp.wait_recv()
    total = gz[0]
    for i in range(1, NZ):
        total = total + gz[i]
    mine = ds(32 * ti + 8 * y, 8)
    gmat[mine, :] = total
    g3 = [send(gmat.at[mine], gmat.at[mine], g_s.at[2, i - 1], g_r.at[2, i - 1], to_y(i)) for i in range(1, NY)]

    start_rs2(0)
    for cp in g3:
        cp.wait_recv()
    g4 = [send(gmat.at[rows], gmat.at[rows], g_s.at[3, i - 1], g_r.at[3, i - 1], dev(z, y, peer_x(i), c)) for i in range(1, NX)]
    g5 = [send(gmat.at[rows], gmat.at[rows], g_s.at[4, 0], g_r.at[4, 0], dev(z, y, x, 1 - c))]
    start_rs2(1)
    for i in range(1, NX):
        g4[i - 1].wait_recv()
        theirs = ds(64 * lax.rem(x + NX - i, NX) + 32 * c, 32)
        g5.append(send(gmat.at[theirs], gmat.at[theirs], g_s.at[4, i], g_r.at[4, i], dev(z, y, x, 1 - c)))
    start_rs2(2)
    for cp in g5:
        cp.wait_recv()
    for cp in g3 + g4 + g5:
        cp.wait_send()
    done = [id(cp) for cp in g3 + g4 + g5]
    pending[:] = [cp for cp in pending if id(cp) not in done]

    def between(j):
        if j == 0:
            for n in order:
                start_ag1(n)
        if j == 2:
            for n in order:
                start_ag2(n)

    cholesky_inverse(gmat, between)
    row = lax.broadcasted_iota(jnp.int32, (RANK, RANK), 0)
    lane = lax.broadcasted_iota(jnp.int32, (RANK, RANK), 1)
    inv = split(jnp.where(row >= lane, gmat[...], 0.0))
    for n in order:
        for cp in ag2[n]:
            cp.wait_recv()
    rt = dot3(inv, split(wf[...]), 1, 0)
    rt_ref[...] = rt
    squares = jnp.sum(rt * rt, axis=1, keepdims=True)
    nbuf[ti] = jnp.broadcast_to(squares, (RANK, 128))
    n1 = [send(nbuf.at[ti], nbuf.at[ti], n_s.at[i], n_r.at[i], p) for i, p in enumerate(tensor_peers)]
    q = dot3(split(pfull[0]), (inv[0][:, :HALF], inv[1][:, :HALF]), 1, 1)
    q_ref[...] = q + dot3(split(pfull[1]), (inv[0][:, HALF:], inv[1][:, HALF:]), 1, 1)
    for cp in n1:
        cp.wait_recv()
    total = nbuf[0]
    for i in range(1, 2 * NX):
        total = total + nbuf[i]
    norm_ref[...] = lax.rsqrt(total / COLS + 1e-06)
    for cp in pending:
        cp.wait_send()


def output_kernel(m_ref, g_ref, wt_ref, q_ref, rt_ref, norm_ref, nm_ref, nw_ref, nr_ref, rh, rl, nh, nl):
    @pl.when(pl.program_id(0) == 0)
    def _():
        rt = rt_ref[...]
        scaled = rt * norm_ref[:, 0:1]
        nr_ref[...] = scaled.T
        rh[...], rl[...] = split(rt)
        nh[...], nl[...] = split(scaled)

    q = split(q_ref[...])
    buf = m_ref[...] + g_ref[...].astype(F32)
    nm_ref[...] = buf - 0.5 * dot3(q, (rh[...], rl[...]), 1, 0)
    step_size = 0.2 * math.sqrt(ROWS / RANK)
    nw_ref[...] = wt_ref[...] - step_size * dot3(q, (nh[...], nl[...]), 1, 0)


def body(momentum, gradient, weights, prior_right):
    vmem = pl.BlockSpec(memory_space=pltpu.VMEM)
    nch = len(CHUNKS)
    dma = pltpu.SemaphoreType.DMA
    q, rt, norm = pl.pallas_call(
        factor_kernel,
        out_shape=(
            jax.ShapeDtypeStruct((BR, RANK), F32),
            jax.ShapeDtypeStruct((RANK, BC), F32),
            jax.ShapeDtypeStruct((RANK, 128), F32),
        ),
        in_specs=[vmem] * 3,
        out_specs=(vmem,) * 3,
        scratch_shapes=[
            pltpu.VMEM((BR, BC), BF16),
            pltpu.VMEM((BR, BC), BF16),
            pltpu.VMEM((2, BR, HALF), F32),
            pltpu.VMEM((2, 256, HALF), F32),
            pltpu.VMEM((2, 256, HALF), F32),
            pltpu.VMEM((2, NX - 1, 64, HALF), F32),
            pltpu.VMEM((2, 64, HALF), F32),
            pltpu.VMEM((2, BR, HALF), F32),
            pltpu.VMEM((RANK, BR), F32),
            pltpu.VMEM((32, RANK), F32),
            pltpu.VMEM((NY - 1, 8, RANK), F32),
            pltpu.VMEM((NZ, 8, RANK), F32),
            pltpu.VMEM((RANK, RANK), F32),
            pltpu.VMEM((RANK, BC), F32),
            pltpu.VMEM((RANK, BC), F32),
            pltpu.VMEM((NY - 1, 64, BC), F32),
            pltpu.VMEM((NZ - 1, 32, BC), F32),
            pltpu.VMEM((64, BC), F32),
            pltpu.VMEM((32, BC), F32),
            pltpu.VMEM((NY - 1, 8, BC), F32),
            pltpu.VMEM((NZ - 1, 8, BC), F32),
            pltpu.VMEM((8, BC), F32),
            pltpu.VMEM((2 * NX, RANK, 128), F32),
            dma((2, 5)), dma((2, 5)),
            dma((2, 2, 3)), dma((2, 2, 3)),
            dma((5, 7)), dma((5, 7)),
            dma((nch, 4, 7)), dma((nch, 4, 7)),
            dma((7,)), dma((7,)),
        ],
        compiler_params=pltpu.CompilerParams(
            collective_id=0, has_side_effects=True, vmem_limit_bytes=50 * 1024 * 1024
        ),
        name="factors",
    )(momentum, gradient, prior_right)
    tile = 128
    by_rows = pl.BlockSpec((tile, BC), lambda i: (i, 0))
    whole = lambda shape: pl.BlockSpec(shape, lambda i: (0, 0))
    return pl.pallas_call(
        output_kernel,
        grid=(BR // tile,),
        out_shape=(
            jax.ShapeDtypeStruct((BR, BC), F32),
            jax.ShapeDtypeStruct((BR, BC), F32),
            jax.ShapeDtypeStruct((BC, RANK), F32),
        ),
        in_specs=[
            by_rows, by_rows, by_rows,
            pl.BlockSpec((tile, RANK), lambda i: (i, 0)),
            whole((RANK, BC)), whole((RANK, 128)),
        ],
        out_specs=(by_rows, by_rows, whole((BC, RANK))),
        scratch_shapes=[pltpu.VMEM((RANK, BC), BF16)] * 4,
        compiler_params=pltpu.CompilerParams(vmem_limit_bytes=50 * 1024 * 1024),
        name="outputs",
    )(momentum, gradient, weights, q, rt, norm)


def solution(mesh):
    in_specs = (P("fsdp", "tensor"), P("fsdp", "tensor"), P("fsdp", "tensor"), P("tensor", None))
    out_specs = (P("fsdp", "tensor"), P("fsdp", "tensor"), P("tensor", None))
    return jax.shard_map(body, mesh=mesh, in_specs=in_specs, out_specs=out_specs, check_vma=False)
```

time: 604 us -> 90.1 us (0.15)
  waiting for transfers between devices: 252 us -> 0 us
  other arithmetic: 240 us -> 0 us
  Pallas kernels: 0 us -> 88 us
  matrix products: 40.3 us -> 0 us
  between operations: 22.6 us -> 0.65 us
  blocking collectives: 17.3 us -> 0 us
  starting transfers between devices: 15 us -> 0 us
  local copies, waits for them, and re-layouts: 12.9 us -> 1.26 us
    another operation x44 -> x0, other arithmetic: 237 us -> none  [the longest x35 180 us: body(): factor = jnp.linalg.cholesky(summed)]
    psum x2 -> x0, waiting for transfers between devices: 229 us -> none  [the longest x1 162 us: body(): right_factor = lax.psum(contract_rows(buffer, ortho_basis), 'fsdp')]
    pallas_call x0 -> x2, Pallas kernels: none -> 88 us  [the longest x1 81.6 us: body(): pl.pallas_call(factor_kernel, out_shape=(jax.ShapeDtypeStruct((BR, RANK),...]
    dot_general x15 -> x0, matrix products: 30.1 us -> none  [the longest x13 23 us: matmul_high(): jnp.dot(left_mat, right_mat, precision=lax.Precision.HIGHEST, preferred_e...]
    ppermute x5 -> x0, waiting for transfers between devices: 23.1 us -> none  [partner_2(): return lax.ppermute(block, axis, route)]
    psum x1 -> x0, blocking collectives: 17.3 us -> none  [body(): totals = lax.psum(jnp.sum(right_factor * right_factor, axis=0), 'tensor')]
    ppermute x5 -> x0, starting transfers between devices: 14.8 us -> none  [partner_2(): return lax.ppermute(block, axis, route)]
    another operation x15 -> x0, matrix products: 10.2 us -> none  [the longest x10 5.32 us: body(): factor = jnp.linalg.cholesky(summed)]
  transfers between devices with their start and end apart: 7 -> 0, of which waited for: 7 -> 0; matrix products, arithmetic and copies ran while one was open for 0% -> 0% of each run, Pallas kernels for 0% -> 0%
where the time goes in v1:
time: 90.1 us; the launch traced here: 89.9 us
  Pallas kernels  88 us (98%)
  local copies, waits for them, and re-layouts  1.26 us (1%)
    pallas_call x1, Pallas kernels, body(): pl.pallas_call(factor_kernel, out_shape=(jax.ShapeDtypeStruct((BR, RANK),...  81.6 us
    pallas_call x1, Pallas kernels, body(): pl.pallas_call(output_kernel, grid=(BR // tile,), out_shape=(jax.ShapeDty...  6.39 us

profile of v1, /device:TPU:1, one launch (start us, length us, event | category | flops | bytes accessed | tf_op | source)
XLA Modules:
  0.0 89.9 jit_solution(718364312824784304)
XLA Ops:
  0.6 0.0 copy-start
  0.6 1.3 %copy-done = bf16[512,1152]{1,0:T(8,128)(2,1)S(1)} copy-done((bf16[512,1152]{1,0:T(8,128)(2,1)S(1)}, bf16[512,1152]{1,0:T(8,128)(2,1)}, u32[]{:S(2)}) %copy-start) | copy-done | bytes 1179672
  1.9 81.6 %factors.1 = (f32[512,256]{1,0:T(8,128)S(1)}, f32[256,1152]{1,0:T(8,128)S(1)}, f32[256,128]{1,0:T(8,128)S(1)}) custom-call(f32[512,1152]{1,0:T(8,128)} %m_ref.3, bf16[512,1152]{1,0:T(8,128)(2,1)S(1)} %copy-done, f32[1152,256]{1,0:T(8,128)} %v_ref.1), custom_call_target="tpu_custom_call" | custom-call | tf_op jit(solution)/shard_map/factors/pallas_call | solution.py:367
  83.5 6.4 %outputs.1 = (f32[512,1152]{1,0:T(8,128)}, f32[512,1152]{1,0:T(8,128)}, f32[1152,256]{1,0:T(8,128)}) custom-call(f32[512,1152]{1,0:T(8,128)} %m_ref.3, bf16[512,1152]{1,0:T(8,128)(2,1)S(1)} %copy-done, f32[512,1152]{1,0:T(8,128)} %wt_ref.1, f32[512,256]{1,0:T(8,128)S(1)} %get-tuple-element.6.q_ref, f32[256,1152]{1,0:T(8,128)S(1)} %get-tuple-element.7.rt_ref, ...), custom_call_target="tpu_custom_call" | custom-call | tf_op jit(solution)/shard_map/outputs/pallas_call | solution.py:414
Async XLA Ops:
  0.6 1.3 %copy-start = (bf16[512,1152]{1,0:T(8,128)(2,1)S(1)}, bf16[512,1152]{1,0:T(8,128)(2,1)}, u32[]{:S(2)}) copy-start(bf16[512,1152]{1,0:T(8,128)(2,1)} %g_ref.3) | copy-start | bytes 3538948

commit v2 on v1

--- a/solution.py
+++ b/solution.py
@@ -20,7 +20,7 @@
 F32 = jnp.float32
 BF16 = jnp.bfloat16
 MESH = pl.DeviceIdType.MESH
-CHUNKS = ((0, 256, "z"), (256, 512, "y"), (768, 384, "y"))
+CHUNKS = ((0, 256, "z"), (256, 384, "y"), (640, 256, "y"), (896, 256, "y"))
 
 
 def dot_f32(a, b, ca, cb):
@@ -39,10 +39,12 @@
 
 
 def dot3(a, b, ca, cb):
-    return dot_bf16(a[0], b[0], ca, cb) + (dot_bf16(a[0], b[1], ca, cb) + dot_bf16(a[1], b[0], ca, cb))
-
-
-def leaf_elimination(block):
+    return dot_bf16(
+        jnp.concatenate([a[0], a[0], a[1]], axis=ca), jnp.concatenate([b[1], b[0], b[0]], axis=cb), ca, cb
+    )
+
+
+def leaf_elimination(block, service):
     n = block.shape[0]
     row = lax.broadcasted_iota(jnp.int32, (n, n), 0)
     lane = lax.broadcasted_iota(jnp.int32, (n, n), 1)
@@ -58,14 +60,15 @@
             cleared = jnp.where((ln == p0 + k) & (rw > p0 + k), 0.0, low)
             low = cleared - f * pivot_row
         block = jnp.concatenate([block[:p0], low], axis=0) if p0 else low
+        service()
     return block
 
 
-def cholesky_inverse(a, between):
+def cholesky_inverse(a, service):
     blocks = RANK // LEAF
     for j in range(blocks):
         s = slice(j * LEAF, (j + 1) * LEAF)
-        d = leaf_elimination(a[s, s])
+        d = leaf_elimination(a[s, s], service)
         row = lax.broadcasted_iota(jnp.int32, (LEAF, LEAF), 0)
         lane = lax.broadcasted_iota(jnp.int32, (LEAF, LEAF), 1)
         pivot = jnp.sum(jnp.where(row == lane, d, 0.0), axis=1, keepdims=True)
@@ -78,15 +81,14 @@
             low = (j + 1) * LEAF
             a[low:, s] = jnp.zeros((RANK - low, LEAF), F32)
             a[low:, :] = a[low:, :] - dot_f32(x[:, low:], a[s, :], 0, 0)
-            between(j)
 
 
 def factor_kernel(
-    m_ref, g_ref, v_ref, q_ref, rt_ref, norm_ref,
-    bh, bl, part, crecv, half, xrecv, own, pfull, pt,
+    m_ref, g_ref, wt_ref, v_ref, nm_ref, wv_ref, q_ref, rh_ref, rl_ref, rtt_ref, norm_ref,
+    mv, gv, vv, bh, bl, part, crecv, half, xrecv, own, pfull, pt,
     gpart, gyrecv, gz, gmat,
     w, wf, r1y, r1z, s1y, s1z, r2y, r2z, s2,
-    nbuf, c_s, c_r, x_s, x_r, g_s, g_r, w_s, w_r, n_s, n_r,
+    nbuf, l_s, c_s, c_r, x_s, x_r, g_s, g_r, w_s, w_r, n_s, n_r,
 ):
     fi, ti = lax.axis_index("fsdp"), lax.axis_index("tensor")
     z, y = fi // NY, lax.rem(fi, NY)
@@ -103,6 +105,9 @@
 
     def peer_x(i):
         return lax.rem(x + i, NX)
+
+    def ds(start, size):
+        return pl.ds(pl.multiple_of(start, size if size < 16 else 16), size)
 
     pending = []
 
@@ -114,32 +119,54 @@
         pending.append(copy)
         return copy
 
+    load_v = pltpu.make_async_copy(v_ref, vv, l_s.at[0])
+    load_v.start()
+    loads = []
+    for k, cc in enumerate((1 - c, c)):
+        rows = ds(256 * cc, 256)
+        loads.append([
+            pltpu.make_async_copy(m_ref.at[rows], mv.at[k], l_s.at[1 + 2 * k]),
+            pltpu.make_async_copy(g_ref.at[rows], gv.at[k], l_s.at[2 + 2 * k]),
+        ])
+        for cp in loads[k]:
+            cp.start()
+
+    load_w = pltpu.make_async_copy(wt_ref, wv_ref, l_s.at[5])
+    load_w.start()
+
     barrier = pltpu.get_barrier_semaphore()
     peers = [dev(z, peer_y(i), x, c) for i in range(1, NY)]
     peers += [dev(peer_z(i), y, x, c) for i in range(1, NZ)]
     tensor_peers = [dev(z, y, x, 1 - c)]
     tensor_peers += [dev(z, y, peer_x(i), cc) for i in range(1, NX) for cc in (c, 1 - c)]
-    for p in peers + tensor_peers:
+    plane_peers = [dev(z, peer_y(j), peer_x(i), c) for i in range(1, NX) for j in range(1, NY)]
+    everyone = peers + tensor_peers + plane_peers
+    for p in everyone:
         pl.semaphore_signal(barrier, inc=1, device_id=p, device_id_type=MESH)
 
-    buf = m_ref[...] + g_ref[...].astype(F32)
-    bh[...], bl[...] = split(buf)
-
-    def ds(start, size):
-        return pl.ds(pl.multiple_of(start, 8), size)
+    load_v.wait()
+    vs = split(vv[...])
+
+    def projected(k, cc):
+        for cp in loads[k]:
+            cp.wait()
+        rows = ds(256 * cc, 256)
+        hi, lo = split(mv[k] + gv[k].astype(F32))
+        bh[rows, :] = hi
+        bl[rows, :] = lo
+        return dot3((hi, lo), vs, 1, 0)
 
     core_rs, x_rs, x_ag, core_ag = [], [], [], []
-    for h in range(2):
-        vh = split(v_ref[:, h * HALF : (h + 1) * HALF])
-        part[h] = dot3((bh[...], bl[...]), vh, 1, 0)
-        if h == 0:
-            pl.semaphore_wait(barrier, len(peers + tensor_peers))
-        core_rs.append(
-            send(part.at[h, ds(256 * (1 - c), 256)], crecv.at[h], c_s.at[h, 0], c_r.at[h, 0], dev(z, y, x, 1 - c))
-        )
+    theirs = projected(0, 1 - c)
+    for h in range(2):
+        part[h] = theirs[:, h * HALF : (h + 1) * HALF]
+    pl.semaphore_wait(barrier, len(everyone))
+    for h in range(2):
+        core_rs.append(send(part.at[h], crecv.at[h], c_s.at[h, 0], c_r.at[h, 0], dev(z, y, x, 1 - c)))
+    ours = projected(1, c)
     for h in range(2):
         core_rs[h].wait_recv()
-        half[h] = part[h, ds(256 * c, 256), :] + crecv[h]
+        half[h] = ours[:, h * HALF : (h + 1) * HALF] + crecv[h]
         x_rs.append([
             send(half.at[h, ds(64 * peer_x(i), 64)], xrecv.at[h, i - 1], x_s.at[h, 0, i - 1], x_r.at[h, 0, i - 1],
                  dev(z, y, peer_x(i), c))
@@ -173,7 +200,8 @@
             cp.wait_recv()
         ph = pfull[h].T
         pt[h * HALF : (h + 1) * HALF, :] = ph
-        w[h * HALF : (h + 1) * HALF, :] = dot3(split(ph), (bh[...], bl[...]), 1, 0)
+        if h == 0:
+            w[:HALF, :] = dot3(split(ph), (bh[...], bl[...]), 1, 0)
 
     rows = ds(32 * ti, 32)
     ptr = pt[rows, :]
@@ -184,6 +212,7 @@
              dev(z, peer_y(i), x, c))
         for i in range(1, NY)
     ]
+    w[HALF:, :] = dot3(split(ph), (bh[...], bl[...]), 1, 0)
 
     def to_y(i):
         return dev(z, peer_y(i), x, c)
@@ -274,10 +303,8 @@
                 send(piece, piece, w_s.at[n, 3, i - 1], w_r.at[n, 3, i - 1], to_z(i)) for i in range(1, NZ)
             ]
 
-    order = range(len(CHUNKS))
-    for n in order:
+    for n in range(len(CHUNKS)):
         start_rs1(n)
-
     for cp in g1:
         cp.wait_recv()
     total = gpart[ds(8 * y, 8), :]
@@ -285,6 +312,9 @@
         total = total + gyrecv[i]
     gz[z] = total
     g2 = [send(gz.at[z], gz.at[z], g_s.at[1, i - 1], g_r.at[1, i - 1], to_z(i)) for i in range(1, NZ)]
+    start_rs2(1)
+    start_rs2(2)
+    start_rs2(0)
     for cp in g2:
         cp.wait_recv()
     total = gz[0]
@@ -292,91 +322,130 @@
         total = total + gz[i]
     mine = ds(32 * ti + 8 * y, 8)
     gmat[mine, :] = total
-    g3 = [send(gmat.at[mine], gmat.at[mine], g_s.at[2, i - 1], g_r.at[2, i - 1], to_y(i)) for i in range(1, NY)]
-
-    start_rs2(0)
-    for cp in g3:
+    g3 = [
+        send(gmat.at[mine], gmat.at[mine], g_s.at[2 + i, j], g_r.at[2 + i, j], dev(z, peer_y(j), peer_x(i), c))
+        for i in range(NX)
+        for j in range(NY)
+        if i or j
+    ]
+    start_rs2(3)
+    start_ag1(1)
+    start_ag1(0)
+    start_ag1(2)
+    g4 = []
+    for i in range(NX):
+        for j in range(NY):
+            if i or j:
+                g3[NY * i + j - 1].wait_recv()
+        block = ds(64 * lax.rem(x + NX - i, NX) + 32 * c, 32)
+        g4.append(send(gmat.at[block], gmat.at[block], g_s.at[6, i], g_r.at[6, i], dev(z, y, x, 1 - c)))
+    start_ag1(3)
+    for cp in g4:
         cp.wait_recv()
-    g4 = [send(gmat.at[rows], gmat.at[rows], g_s.at[3, i - 1], g_r.at[3, i - 1], dev(z, y, peer_x(i), c)) for i in range(1, NX)]
-    g5 = [send(gmat.at[rows], gmat.at[rows], g_s.at[4, 0], g_r.at[4, 0], dev(z, y, x, 1 - c))]
-    start_rs2(1)
-    for i in range(1, NX):
-        g4[i - 1].wait_recv()
-        theirs = ds(64 * lax.rem(x + NX - i, NX) + 32 * c, 32)
-        g5.append(send(gmat.at[theirs], gmat.at[theirs], g_s.at[4, i], g_r.at[4, i], dev(z, y, x, 1 - c)))
-    start_rs2(2)
-    for cp in g5:
-        cp.wait_recv()
-    for cp in g3 + g4 + g5:
+    for cp in g3 + g4:
         cp.wait_send()
-    done = [id(cp) for cp in g3 + g4 + g5]
+    done = [id(cp) for cp in g3 + g4]
     pending[:] = [cp for cp in pending if id(cp) not in done]
 
-    def between(j):
-        if j == 0:
-            for n in order:
-                start_ag1(n)
-        if j == 2:
-            for n in order:
-                start_ag2(n)
-
-    cholesky_inverse(gmat, between)
+    plan = {
+        0: [(start_ag2, 0)],
+        2: [(start_ag2, 1)],
+        4: [(start_ag2, 2)],
+        8: [(start_ag2, 3)],
+    }
+    panels = []
+
+    def service():
+        for step, n in plan.get(len(panels), ()):
+            step(n)
+        panels.append(0)
+
+    cholesky_inverse(gmat, service)
     row = lax.broadcasted_iota(jnp.int32, (RANK, RANK), 0)
     lane = lax.broadcasted_iota(jnp.int32, (RANK, RANK), 1)
     inv = split(jnp.where(row >= lane, gmat[...], 0.0))
-    for n in order:
+    q = dot3(split(pfull[0]), (inv[0][:, :HALF], inv[1][:, :HALF]), 1, 1)
+    q = q + dot3(split(pfull[1]), (inv[0][:, HALF:], inv[1][:, HALF:]), 1, 1)
+    for n in range(len(CHUNKS)):
         for cp in ag2[n]:
             cp.wait_recv()
     rt = dot3(inv, split(wf[...]), 1, 0)
-    rt_ref[...] = rt
-    squares = jnp.sum(rt * rt, axis=1, keepdims=True)
-    nbuf[ti] = jnp.broadcast_to(squares, (RANK, 128))
+    squares = rt[:, :128] * rt[:, :128]
+    for k in range(1, BC // 128):
+        piece = rt[:, k * 128 : (k + 1) * 128]
+        squares = squares + piece * piece
+    squares = squares.T
+    total = squares[0:8, :]
+    for k in range(1, 16):
+        total = total + squares[8 * k : 8 * k + 8, :]
+    nbuf[ti] = total
     n1 = [send(nbuf.at[ti], nbuf.at[ti], n_s.at[i], n_r.at[i], p) for i, p in enumerate(tensor_peers)]
-    q = dot3(split(pfull[0]), (inv[0][:, :HALF], inv[1][:, :HALF]), 1, 1)
-    q_ref[...] = q + dot3(split(pfull[1]), (inv[0][:, HALF:], inv[1][:, HALF:]), 1, 1)
+    rsplit = split(rt)
+    rh_ref[...], rl_ref[...] = rsplit
+    for k in range(2):
+        rows = ds(256 * (1 - c if k == 0 else c), 256)
+        qk = jnp.where(c == k, q[256:], q[:256])
+        nm_ref[rows, :] = mv[k] + gv[k].astype(F32) - dot3(split(0.5 * qk), rsplit, 1, 0)
+    rtt_ref[...] = rt.T
     for cp in n1:
         cp.wait_recv()
     total = nbuf[0]
     for i in range(1, 2 * NX):
         total = total + nbuf[i]
-    norm_ref[...] = lax.rsqrt(total / COLS + 1e-06)
+    total = jnp.sum(total, axis=0, keepdims=True)
+    scale = lax.rsqrt(total / COLS + 1e-06)
+    norm_ref[...] = jnp.broadcast_to(scale, (8, RANK))
+    q_ref[...] = q * (scale * (0.2 * math.sqrt(ROWS / RANK)))
+    load_w.wait()
     for cp in pending:
         cp.wait_send()
 
 
-def output_kernel(m_ref, g_ref, wt_ref, q_ref, rt_ref, norm_ref, nm_ref, nw_ref, nr_ref, rh, rl, nh, nl):
-    @pl.when(pl.program_id(0) == 0)
-    def _():
-        rt = rt_ref[...]
-        scaled = rt * norm_ref[:, 0:1]
-        nr_ref[...] = scaled.T
-        rh[...], rl[...] = split(rt)
-        nh[...], nl[...] = split(scaled)
-
-    q = split(q_ref[...])
-    buf = m_ref[...] + g_ref[...].astype(F32)
-    nm_ref[...] = buf - 0.5 * dot3(q, (rh[...], rl[...]), 1, 0)
-    step_size = 0.2 * math.sqrt(ROWS / RANK)
-    nw_ref[...] = wt_ref[...] - step_size * dot3(q, (nh[...], nl[...]), 1, 0)
+def output_kernel(nm_ref, wv_ref, q_ref, rh_ref, rl_ref, rtt_ref, norm_ref, onm_ref, onw_ref, onr_ref, nw, nr, sems):
+    copies = [pltpu.make_async_copy(nm_ref, onm_ref, sems.at[0])]
+    copies[0].start()
+    nr[...] = rtt_ref[...] * norm_ref[0:1, :]
+    copies.append(pltpu.make_async_copy(nr, onr_ref, sems.at[1]))
+    copies[1].start()
+    right = (rh_ref[...], rl_ref[...])
+    for k in range(2):
+        rows = pl.ds(256 * k, 256)
+        nw[rows, :] = wv_ref[rows, :] - dot3(split(q_ref[rows, :]), right, 1, 0)
+        copies.append(pltpu.make_async_copy(nw.at[rows], onw_ref.at[rows], sems.at[2 + k]))
+        copies[2 + k].start()
+    for cp in copies:
+        cp.wait()
+
+
+def hbm(array):
+    return pltpu.with_memory_space_constraint(array, pltpu.HBM)
 
 
 def body(momentum, gradient, weights, prior_right):
     vmem = pl.BlockSpec(memory_space=pltpu.VMEM)
     nch = len(CHUNKS)
     dma = pltpu.SemaphoreType.DMA
-    q, rt, norm = pl.pallas_call(
+    inner = (
+        pltpu.VMEM((BR, BC), F32),
+        pltpu.VMEM((BR, BC), F32),
+        pltpu.VMEM((BR, RANK), F32),
+        pltpu.VMEM((RANK, BC), BF16),
+        pltpu.VMEM((RANK, BC), BF16),
+        pltpu.VMEM((BC, RANK), F32),
+        pltpu.VMEM((8, RANK), F32),
+    )
+    factors = pl.pallas_call(
         factor_kernel,
-        out_shape=(
-            jax.ShapeDtypeStruct((BR, RANK), F32),
-            jax.ShapeDtypeStruct((RANK, BC), F32),
-            jax.ShapeDtypeStruct((RANK, 128), F32),
-        ),
-        in_specs=[vmem] * 3,
-        out_specs=(vmem,) * 3,
+        out_shape=inner,
+        in_specs=[pl.BlockSpec(memory_space=pltpu.HBM)] * 4,
+        out_specs=(vmem,) * len(inner),
         scratch_shapes=[
+            pltpu.VMEM((2, 256, BC), F32),
+            pltpu.VMEM((2, 256, BC), BF16),
+            pltpu.VMEM((BC, RANK), F32),
             pltpu.VMEM((BR, BC), BF16),
             pltpu.VMEM((BR, BC), BF16),
-            pltpu.VMEM((2, BR, HALF), F32),
+            pltpu.VMEM((2, 256, HALF), F32),
             pltpu.VMEM((2, 256, HALF), F32),
             pltpu.VMEM((2, 256, HALF), F32),
             pltpu.VMEM((2, NX - 1, 64, HALF), F32),
@@ -396,39 +465,32 @@
             pltpu.VMEM((NY - 1, 8, BC), F32),
             pltpu.VMEM((NZ - 1, 8, BC), F32),
             pltpu.VMEM((8, BC), F32),
-            pltpu.VMEM((2 * NX, RANK, 128), F32),
+            pltpu.VMEM((2 * NX, 8, RANK), F32),
+            dma((6,)),
             dma((2, 5)), dma((2, 5)),
             dma((2, 2, 3)), dma((2, 2, 3)),
-            dma((5, 7)), dma((5, 7)),
+            dma((7, 7)), dma((7, 7)),
             dma((nch, 4, 7)), dma((nch, 4, 7)),
             dma((7,)), dma((7,)),
         ],
         compiler_params=pltpu.CompilerParams(
-            collective_id=0, has_side_effects=True, vmem_limit_bytes=50 * 1024 * 1024
+            collective_id=0, has_side_effects=True, vmem_limit_bytes=40 * 1024 * 1024
         ),
         name="factors",
-    )(momentum, gradient, prior_right)
-    tile = 128
-    by_rows = pl.BlockSpec((tile, BC), lambda i: (i, 0))
-    whole = lambda shape: pl.BlockSpec(shape, lambda i: (0, 0))
+    )(hbm(momentum), hbm(gradient), hbm(weights), hbm(prior_right))
     return pl.pallas_call(
         output_kernel,
-        grid=(BR // tile,),
         out_shape=(
             jax.ShapeDtypeStruct((BR, BC), F32),
             jax.ShapeDtypeStruct((BR, BC), F32),
             jax.ShapeDtypeStruct((BC, RANK), F32),
         ),
-        in_specs=[
-            by_rows, by_rows, by_rows,
-            pl.BlockSpec((tile, RANK), lambda i: (i, 0)),
-            whole((RANK, BC)), whole((RANK, 128)),
-        ],
-        out_specs=(by_rows, by_rows, whole((BC, RANK))),
-        scratch_shapes=[pltpu.VMEM((RANK, BC), BF16)] * 4,
-        compiler_params=pltpu.CompilerParams(vmem_limit_bytes=50 * 1024 * 1024),
+        in_specs=[vmem] * len(inner),
+        out_specs=(pl.BlockSpec(memory_space=pltpu.HBM),) * 3,
+        scratch_shapes=[pltpu.VMEM((BR, BC), F32), pltpu.VMEM((BC, RANK), F32), dma((4,))],
+        compiler_params=pltpu.CompilerParams(vmem_limit_bytes=40 * 1024 * 1024),
         name="outputs",
-    )(momentum, gradient, weights, q, rt, norm)
+    )(*[pltpu.with_memory_space_constraint(a, pltpu.VMEM) for a in factors])
 
 
 def solution(mesh):

time: 90.1 us -> 69.3 us (0.77)
  Pallas kernels: 88 us -> 68.4 us
  local copies, waits for them, and re-layouts: 1.26 us -> 0 us
    pallas_call x2, Pallas kernels: 88 us -> 68.4 us  [the longest x1 65.8 us: body(): pl.pallas_call(factor_kernel, out_shape=inner, in_specs=[pl.BlockSpec(mem...]
    unnamed x2 -> x0, local copies, waits for them, and re-layouts: 1.26 us -> none
where the time goes in v2:
time: 69.3 us; the launch traced here: 69.2 us
  Pallas kernels  68.4 us (99%)
  between operations  0.8 us (1%)
    pallas_call x1, Pallas kernels, body(): pl.pallas_call(factor_kernel, out_shape=inner, in_specs=[pl.BlockSpec(mem...  65.8 us
    pallas_call x1, Pallas kernels, body(): pl.pallas_call(output_kernel, out_shape=(jax.ShapeDtypeStruct((BR, BC), F...  2.67 us

profile of v2, /device:TPU:1, one launch (start us, length us, event | category | flops | bytes accessed | tf_op | source)
XLA Modules:
  0.0 69.2 jit_solution(7499883321890359635)
XLA Ops:
  0.6 65.8 %factors.1 = (f32[512,1152]{1,0:T(8,128)S(1)}, f32[512,1152]{1,0:T(8,128)S(1)}, f32[512,256]{1,0:T(8,128)S(1)}, bf16[256,1152]{1,0:T(8,128)(2,1)S(1)}, bf16[256,...) custom-call(f32[512,1152]{1,0:T(8,128)} %m_ref.1, bf16[512,1152]{1,0:T(8,128)(2,1)} %g_ref.1, ...), custom_call_target="tpu_custom_call" | custom-call | tf_op jit(solution)/shard_map/factors/pallas_call | solution.py:437
  66.4 2.7 %outputs.1 = (f32[512,1152]{1,0:T(8,128)}, f32[512,1152]{1,0:T(8,128)}, f32[1152,256]{1,0:T(8,128)}) custom-call(f32[512,1152]{1,0:T(8,128)S(1)} %get-tuple-element.10.nm_ref, f32[512,1152]{1,0:T(8,128)S(1)} %get-tuple-element.11.wv_ref, f32[512,256]{1,0:T(8,128)S(1)} %get-tuple-element.12.q_ref, bf16[256,1152]{1,0:T(8,128)(2,1)S(1)} %get-tuple-element.13.rh_ref, ...), custom_call_target="tpu_custom_call" | custom-call | tf_op jit(solution)/shard_map/outputs/pallas_call | solution.py:481

commit v3 on v2

--- a/solution.py
+++ b/solution.py
@@ -20,7 +20,7 @@
 F32 = jnp.float32
 BF16 = jnp.bfloat16
 MESH = pl.DeviceIdType.MESH
-CHUNKS = ((0, 256, "z"), (256, 384, "y"), (640, 256, "y"), (896, 256, "y"))
+CHUNKS = ((0, 256, "z"), (256, 128, "y"), (384, 256, "y"), (640, 256, "y"), (896, 256, "y"))
 
 
 def dot_f32(a, b, ca, cb):
@@ -86,7 +86,7 @@
 def factor_kernel(
     m_ref, g_ref, wt_ref, v_ref, nm_ref, wv_ref, q_ref, rh_ref, rl_ref, rtt_ref, norm_ref,
     mv, gv, vv, bh, bl, part, crecv, half, xrecv, own, pfull, pt,
-    gpart, gyrecv, gz, gmat,
+    gpart, gyrecv, gz, gsum, gmat,
     w, wf, r1y, r1z, s1y, s1z, r2y, r2z, s2,
     nbuf, l_s, c_s, c_r, x_s, x_r, g_s, g_r, w_s, w_r, n_s, n_r,
 ):
@@ -111,13 +111,19 @@
 
     pending = []
 
-    def send(src, dst, ss, rs, to):
-        copy = pltpu.make_async_remote_copy(
-            src_ref=src, dst_ref=dst, send_sem=ss, recv_sem=rs, device_id=to, device_id_type=MESH
+    def send(copies, sems, size):
+        for src, dst, to in copies:
+            pltpu.make_async_remote_copy(
+                src_ref=src, dst_ref=dst, send_sem=sems[0], recv_sem=sems[1], device_id=to, device_id_type=MESH
+            ).start()
+        group = pltpu.make_async_remote_copy(
+            src_ref=size, dst_ref=size, send_sem=sems[0], recv_sem=sems[1], device_id=copies[0][2], device_id_type=MESH
         )
-        copy.start()
-        pending.append(copy)
-        return copy
+        pending.append(group)
+        return group
+
+    def both(sem_s, sem_r, *at):
+        return sem_s.at[at], sem_r.at[at]
 
     load_v = pltpu.make_async_copy(v_ref, vv, l_s.at[0])
     load_v.start()
@@ -131,9 +137,6 @@
         for cp in loads[k]:
             cp.start()
 
-    load_w = pltpu.make_async_copy(wt_ref, wv_ref, l_s.at[5])
-    load_w.start()
-
     barrier = pltpu.get_barrier_semaphore()
     peers = [dev(z, peer_y(i), x, c) for i in range(1, NY)]
     peers += [dev(peer_z(i), y, x, c) for i in range(1, NZ)]
@@ -156,48 +159,38 @@
         bl[rows, :] = lo
         return dot3((hi, lo), vs, 1, 0)
 
-    core_rs, x_rs, x_ag, core_ag = [], [], [], []
+    other = dev(z, y, x, 1 - c)
+    x_peers = [(i, dev(z, y, peer_x(i), c)) for i in range(1, NX)]
+    core_rs, x_rs, x_ag = [], [], []
     theirs = projected(0, 1 - c)
     for h in range(2):
         part[h] = theirs[:, h * HALF : (h + 1) * HALF]
     pl.semaphore_wait(barrier, len(everyone))
     for h in range(2):
-        core_rs.append(send(part.at[h], crecv.at[h], c_s.at[h, 0], c_r.at[h, 0], dev(z, y, x, 1 - c)))
+        core_rs.append(send([(part.at[h], crecv.at[h], other)], both(c_s, c_r, h, 0), crecv.at[h]))
     ours = projected(1, c)
+    load_w = pltpu.make_async_copy(wt_ref, wv_ref, l_s.at[5])
+    load_w.start()
     for h in range(2):
         core_rs[h].wait_recv()
         half[h] = ours[:, h * HALF : (h + 1) * HALF] + crecv[h]
-        x_rs.append([
-            send(half.at[h, ds(64 * peer_x(i), 64)], xrecv.at[h, i - 1], x_s.at[h, 0, i - 1], x_r.at[h, 0, i - 1],
-                 dev(z, y, peer_x(i), c))
-            for i in range(1, NX)
-        ])
-    for h in range(2):
-        for cp in x_rs[h]:
-            cp.wait_recv()
+        x_rs.append(send(
+            [(half.at[h, ds(64 * peer_x(i), 64)], xrecv.at[h, i - 1], to) for i, to in x_peers],
+            both(x_s, x_r, h, 0), xrecv.at[h],
+        ))
+    for h in range(2):
+        x_rs[h].wait_recv()
         total = half[h, ds(64 * x, 64), :]
         for i in range(NX - 1):
             total = total + xrecv[h, i]
         own[h] = total
-        at = 256 * c + 64 * x
-        x_ag.append([
-            send(own.at[h], pfull.at[h, ds(at, 64)], x_s.at[h, 1, i - 1], x_r.at[h, 1, i - 1], dev(z, y, peer_x(i), c))
-            for i in range(1, NX)
-        ])
-        core_ag.append([
-            send(own.at[h], pfull.at[h, ds(at, 64)], c_s.at[h, 1], c_r.at[h, 1], dev(z, y, x, 1 - c))
-        ])
-        pfull[h, ds(at, 64), :] = total
-    for h in range(2):
-        for i in range(1, NX):
-            x_ag[h][i - 1].wait_recv()
-            at = 256 * c + 64 * lax.rem(x + NX - i, NX)
-            core_ag[h].append(
-                send(pfull.at[h, ds(at, 64)], pfull.at[h, ds(at, 64)], c_s.at[h, 1 + i], c_r.at[h, 1 + i],
-                     dev(z, y, x, 1 - c))
-            )
-        for cp in core_ag[h]:
-            cp.wait_recv()
+        piece = pfull.at[h, ds(256 * c + 64 * x, 64)]
+        x_ag.append(send([(own.at[h], piece, to) for _, to in x_peers], both(x_s, x_r, h, 1), xrecv.at[h]))
+        pfull[h, ds(256 * c + 64 * x, 64), :] = total
+    for h in range(2):
+        x_ag[h].wait_recv()
+        piece = pfull.at[h, ds(256 * c, 256)]
+        send([(piece, piece, other)], both(c_s, c_r, h, 1), piece).wait_recv()
         ph = pfull[h].T
         pt[h * HALF : (h + 1) * HALF, :] = ph
         if h == 0:
@@ -207,151 +200,123 @@
     ptr = pt[rows, :]
     for h in range(2):
         gpart[:, h * HALF : (h + 1) * HALF] = dot_f32(ptr, pfull[h], 1, 0)
-    g1 = [
-        send(gpart.at[ds(8 * peer_y(i), 8)], gyrecv.at[i - 1], g_s.at[0, i - 1], g_r.at[0, i - 1],
-             dev(z, peer_y(i), x, c))
-        for i in range(1, NY)
-    ]
+    g1 = send(
+        [(gpart.at[ds(8 * peer_y(i), 8)], gyrecv.at[i - 1], dev(z, peer_y(i), x, c)) for i in range(1, NY)],
+        both(g_s, g_r, 0), gyrecv,
+    )
     w[HALF:, :] = dot3(split(ph), (bh[...], bl[...]), 1, 0)
 
-    def to_y(i):
-        return dev(z, peer_y(i), x, c)
-
-    def to_z(i):
-        return dev(peer_z(i), y, x, c)
-
+    y_peers = [(i, dev(z, peer_y(i), x, c)) for i in range(1, NY)]
+    z_peers = [(i, dev(peer_z(i), y, x, c)) for i in range(1, NZ)]
     rs1, rs2, ag1, ag2 = {}, {}, {}, {}
 
     def start_rs1(n):
         c0, nc, first = CHUNKS[n]
         cs = pl.ds(c0, nc)
+        sems = both(w_s, w_r, n, 0)
         if first == "y":
-            rs1[n] = [
-                send(w.at[ds(64 * peer_y(i), 64), cs], r1y.at[i - 1, :, cs], w_s.at[n, 0, i - 1], w_r.at[n, 0, i - 1], to_y(i))
-                for i in range(1, NY)
-            ]
+            rs1[n] = send(
+                [(w.at[ds(64 * peer_y(i), 64), cs], r1y.at[i - 1, :, cs], to) for i, to in y_peers], sems, r1y.at[:, :, cs]
+            )
         else:
-            rs1[n] = [
-                send(w.at[ds(32 * peer_z(i), 32), cs], r1z.at[i - 1, :, cs], w_s.at[n, 0, i - 1], w_r.at[n, 0, i - 1], to_z(i))
-                for i in range(1, NZ)
-            ]
+            rs1[n] = send(
+                [(w.at[ds(32 * peer_z(i), 32), cs], r1z.at[i - 1, :, cs], to) for i, to in z_peers], sems, r1z.at[:, :, cs]
+            )
 
     def start_rs2(n):
         c0, nc, first = CHUNKS[n]
         cs = pl.ds(c0, nc)
-        for cp in rs1[n]:
-            cp.wait_recv()
+        sems = both(w_s, w_r, n, 1)
+        rs1[n].wait_recv()
         if first == "y":
             total = w[ds(64 * y, 64), cs]
             for i in range(NY - 1):
                 total = total + r1y[i, :, cs]
             s1y[:, cs] = total
-            rs2[n] = [
-                send(s1y.at[ds(8 * peer_z(i), 8), cs], r2z.at[i - 1, :, cs], w_s.at[n, 1, i - 1], w_r.at[n, 1, i - 1], to_z(i))
-                for i in range(1, NZ)
-            ]
+            rs2[n] = send(
+                [(s1y.at[ds(8 * peer_z(i), 8), cs], r2z.at[i - 1, :, cs], to) for i, to in z_peers], sems, r2z.at[:, :, cs]
+            )
         else:
             total = w[ds(32 * z, 32), cs]
             for i in range(NZ - 1):
                 total = total + r1z[i, :, cs]
             s1z[:, cs] = total
-            rs2[n] = [
-                send(s1z.at[ds(8 * peer_y(i), 8), cs], r2y.at[i - 1, :, cs], w_s.at[n, 1, i - 1], w_r.at[n, 1, i - 1], to_y(i))
-                for i in range(1, NY)
-            ]
+            rs2[n] = send(
+                [(s1z.at[ds(8 * peer_y(i), 8), cs], r2y.at[i - 1, :, cs], to) for i, to in y_peers], sems, r2y.at[:, :, cs]
+            )
 
     def start_ag1(n):
         c0, nc, first = CHUNKS[n]
         cs = pl.ds(c0, nc)
-        for cp in rs2[n]:
-            cp.wait_recv()
+        sems = both(w_s, w_r, n, 2)
+        rs2[n].wait_recv()
         if first == "y":
             total = s1y[ds(8 * z, 8), cs]
             for i in range(NZ - 1):
                 total = total + r2z[i, :, cs]
-            at = 64 * y + 8 * z
-            s2[:, cs] = total
-            ag1[n] = [
-                send(s2.at[:, cs], wf.at[ds(at, 8), cs], w_s.at[n, 2, i - 1], w_r.at[n, 2, i - 1], to_z(i))
-                for i in range(1, NZ)
-            ]
+            piece, to_all, size = wf.at[ds(64 * y + 8 * z, 8), cs], z_peers, r2z.at[:, :, cs]
         else:
             total = s1z[ds(8 * y, 8), cs]
             for i in range(NY - 1):
                 total = total + r2y[i, :, cs]
-            at = 32 * z + 8 * y
-            s2[:, cs] = total
-            ag1[n] = [
-                send(s2.at[:, cs], wf.at[ds(at, 8), cs], w_s.at[n, 2, i - 1], w_r.at[n, 2, i - 1], to_y(i))
-                for i in range(1, NY)
-            ]
-        wf[ds(at, 8), cs] = total
+            piece, to_all, size = wf.at[ds(32 * z + 8 * y, 8), cs], y_peers, r2y.at[:, :, cs]
+        s2[:, cs] = total
+        ag1[n] = send([(s2.at[:, cs], piece, to) for _, to in to_all], sems, size)
+        piece[...] = total
 
     def start_ag2(n):
         c0, nc, first = CHUNKS[n]
         cs = pl.ds(c0, nc)
-        for cp in ag1[n]:
-            cp.wait_recv()
+        sems = both(w_s, w_r, n, 3)
+        ag1[n].wait_recv()
         if first == "y":
-            piece = wf.at[ds(64 * y, 64), cs]
-            ag2[n] = [
-                send(piece, piece, w_s.at[n, 3, i - 1], w_r.at[n, 3, i - 1], to_y(i)) for i in range(1, NY)
-            ]
+            piece, to_all, size = wf.at[ds(64 * y, 64), cs], y_peers, r1y.at[:, :, cs]
         else:
-            piece = wf.at[ds(32 * z, 32), cs]
-            ag2[n] = [
-                send(piece, piece, w_s.at[n, 3, i - 1], w_r.at[n, 3, i - 1], to_z(i)) for i in range(1, NZ)
-            ]
+            piece, to_all, size = wf.at[ds(32 * z, 32), cs], z_peers, r1z.at[:, :, cs]
+        ag2[n] = send([(piece, piece, to) for _, to in to_all], sems, size)
 
     for n in range(len(CHUNKS)):
         start_rs1(n)
-    for cp in g1:
-        cp.wait_recv()
+    g1.wait_recv()
     total = gpart[ds(8 * y, 8), :]
     for i in range(NY - 1):
         total = total + gyrecv[i]
     gz[z] = total
-    g2 = [send(gz.at[z], gz.at[z], g_s.at[1, i - 1], g_r.at[1, i - 1], to_z(i)) for i in range(1, NZ)]
+    g2 = send([(gz.at[z], gz.at[z], to) for _, to in z_peers], both(g_s, g_r, 1), gz.at[pl.ds(0, NZ - 1)])
     start_rs2(1)
     start_rs2(2)
+    start_rs2(3)
     start_rs2(0)
-    for cp in g2:
-        cp.wait_recv()
+    g2.wait_recv()
     total = gz[0]
     for i in range(1, NZ):
         total = total + gz[i]
-    mine = ds(32 * ti + 8 * y, 8)
-    gmat[mine, :] = total
-    g3 = [
-        send(gmat.at[mine], gmat.at[mine], g_s.at[2 + i, j], g_r.at[2 + i, j], dev(z, peer_y(j), peer_x(i), c))
-        for i in range(NX)
-        for j in range(NY)
-        if i or j
-    ]
-    start_rs2(3)
+    mine = gsum.at[x, c, ds(8 * y, 8)]
+    mine[...] = total
+    g3 = send(
+        [(mine, mine, dev(z, peer_y(j), peer_x(i), c)) for i in range(NX) for j in range(NY) if i or j],
+        both(g_s, g_r, 2), w.at[pl.ds(0, 8 * (NX * NY - 1)), pl.ds(0, RANK)],
+    )
     start_ag1(1)
+    start_rs2(4)
     start_ag1(0)
     start_ag1(2)
-    g4 = []
+    g3.wait_recv()
+    ours = gsum.at[:, c]
+    g4 = send([(ours, ours, other)], both(g_s, g_r, 3), ours)
+    start_ag1(3)
+    start_ag2(1)
+    start_ag2(0)
+    start_ag1(4)
+    g4.wait_recv()
     for i in range(NX):
-        for j in range(NY):
-            if i or j:
-                g3[NY * i + j - 1].wait_recv()
-        block = ds(64 * lax.rem(x + NX - i, NX) + 32 * c, 32)
-        g4.append(send(gmat.at[block], gmat.at[block], g_s.at[6, i], g_r.at[6, i], dev(z, y, x, 1 - c)))
-    start_ag1(3)
-    for cp in g4:
-        cp.wait_recv()
-    for cp in g3 + g4:
-        cp.wait_send()
-    done = [id(cp) for cp in g3 + g4]
-    pending[:] = [cp for cp in pending if id(cp) not in done]
+        for k in range(2):
+            gmat[64 * i + 32 * k : 64 * i + 32 * k + 32, :] = gsum[i, k]
 
     plan = {
-        0: [(start_ag2, 0)],
-        2: [(start_ag2, 1)],
-        4: [(start_ag2, 2)],
-        8: [(start_ag2, 3)],
+        2: [(start_ag2, 2)],
+        5: [(start_ag2, 3)],
+        9: [(start_ag2, 4)],
     }
     panels = []
 
@@ -367,8 +332,7 @@
     q = dot3(split(pfull[0]), (inv[0][:, :HALF], inv[1][:, :HALF]), 1, 1)
     q = q + dot3(split(pfull[1]), (inv[0][:, HALF:], inv[1][:, HALF:]), 1, 1)
     for n in range(len(CHUNKS)):
-        for cp in ag2[n]:
-            cp.wait_recv()
+        ag2[n].wait_recv()
     rt = dot3(inv, split(wf[...]), 1, 0)
     squares = rt[:, :128] * rt[:, :128]
     for k in range(1, BC // 128):
@@ -379,7 +343,7 @@
     for k in range(1, 16):
         total = total + squares[8 * k : 8 * k + 8, :]
     nbuf[ti] = total
-    n1 = [send(nbuf.at[ti], nbuf.at[ti], n_s.at[i], n_r.at[i], p) for i, p in enumerate(tensor_peers)]
+    n1 = send([(nbuf.at[ti], nbuf.at[ti], p) for p in tensor_peers], both(n_s, n_r, 0), nbuf.at[pl.ds(0, 2 * NX - 1)])
     rsplit = split(rt)
     rh_ref[...], rl_ref[...] = rsplit
     for k in range(2):
@@ -387,8 +351,7 @@
         qk = jnp.where(c == k, q[256:], q[:256])
         nm_ref[rows, :] = mv[k] + gv[k].astype(F32) - dot3(split(0.5 * qk), rsplit, 1, 0)
     rtt_ref[...] = rt.T
-    for cp in n1:
-        cp.wait_recv()
+    n1.wait_recv()
     total = nbuf[0]
     for i in range(1, 2 * NX):
         total = total + nbuf[i]
@@ -423,7 +386,6 @@
 
 def body(momentum, gradient, weights, prior_right):
     vmem = pl.BlockSpec(memory_space=pltpu.VMEM)
-    nch = len(CHUNKS)
     dma = pltpu.SemaphoreType.DMA
     inner = (
         pltpu.VMEM((BR, BC), F32),
@@ -455,6 +417,7 @@
             pltpu.VMEM((32, RANK), F32),
             pltpu.VMEM((NY - 1, 8, RANK), F32),
             pltpu.VMEM((NZ, 8, RANK), F32),
+            pltpu.VMEM((NX, 2, 32, RANK), F32),
             pltpu.VMEM((RANK, RANK), F32),
             pltpu.VMEM((RANK, BC), F32),
             pltpu.VMEM((RANK, BC), F32),
@@ -467,11 +430,11 @@
             pltpu.VMEM((8, BC), F32),
             pltpu.VMEM((2 * NX, 8, RANK), F32),
             dma((6,)),
-            dma((2, 5)), dma((2, 5)),
-            dma((2, 2, 3)), dma((2, 2, 3)),
-            dma((7, 7)), dma((7, 7)),
-            dma((nch, 4, 7)), dma((nch, 4, 7)),
-            dma((7,)), dma((7,)),
+            dma((2, 2)), dma((2, 2)),
+            dma((2, 2)), dma((2, 2)),
+            dma((4,)), dma((4,)),
+            dma((len(CHUNKS), 4)), dma((len(CHUNKS), 4)),
+            dma((1,)), dma((1,)),
         ],
         compiler_params=pltpu.CompilerParams(
             collective_id=0, has_side_effects=True, vmem_limit_bytes=40 * 1024 * 1024

time: 69.3 us -> 66.3 us (0.957)
  Pallas kernels: 68.4 us -> 65.6 us
    pallas_call x1, Pallas kernels: 65.8 us -> 62.9 us  [body(): pl.pallas_call(factor_kernel, out_shape=inner, in_specs=[pl.BlockSpec(mem...]
where the time goes in v3:
time: 66.3 us; the launch traced here: 66.2 us
  Pallas kernels  65.6 us (99%)
    pallas_call x1, Pallas kernels, body(): pl.pallas_call(factor_kernel, out_shape=inner, in_specs=[pl.BlockSpec(mem...  62.9 us
    pallas_call x1, Pallas kernels, body(): pl.pallas_call(output_kernel, out_shape=(jax.ShapeDtypeStruct((BR, BC), F...  2.67 us

profile of v3, /device:TPU:1, one launch (start us, length us, event | category | flops | bytes accessed | tf_op | source)
XLA Modules:
  0.0 66.2 jit_solution(13175569104486624576)
XLA Ops:
  0.6 62.9 %factors.1 = (f32[512,1152]{1,0:T(8,128)S(1)}, f32[512,1152]{1,0:T(8,128)S(1)}, f32[512,256]{1,0:T(8,128)S(1)}, bf16[256,1152]{1,0:T(8,128)(2,1)S(1)}, bf16[256,...) custom-call(f32[512,1152]{1,0:T(8,128)} %m_ref.1, bf16[512,1152]{1,0:T(8,128)(2,1)} %g_ref.1, ...), custom_call_target="tpu_custom_call" | custom-call | tf_op jit(solution)/shard_map/factors/pallas_call | solution.py:399
  63.6 2.7 %outputs.1 = (f32[512,1152]{1,0:T(8,128)}, f32[512,1152]{1,0:T(8,128)}, f32[1152,256]{1,0:T(8,128)}) custom-call(f32[512,1152]{1,0:T(8,128)S(1)} %get-tuple-element.10.nm_ref, f32[512,1152]{1,0:T(8,128)S(1)} %get-tuple-element.11.wv_ref, f32[512,256]{1,0:T(8,128)S(1)} %get-tuple-element.12.q_ref, bf16[256,1152]{1,0:T(8,128)(2,1)S(1)} %get-tuple-element.13.rh_ref, ...), custom_call_target="tpu_custom_call" | custom-call | tf_op jit(solution)/shard_map/outputs/pallas_call | solution.py:444

commit v4 on v3

--- a/solution.py
+++ b/solution.py
@@ -20,7 +20,7 @@
 F32 = jnp.float32
 BF16 = jnp.bfloat16
 MESH = pl.DeviceIdType.MESH
-CHUNKS = ((0, 256, "z"), (256, 128, "y"), (384, 256, "y"), (640, 256, "y"), (896, 256, "y"))
+CHUNKS = ((0, 256, "z"), (256, 256, "y"), (512, 256, "y"), (768, 256, "y"), (1024, 128, "y"))
 
 
 def dot_f32(a, b, ca, cb):
@@ -53,12 +53,12 @@
         rw, ln, low = row[p0:], lane[p0:], block[p0:]
         for k in range(PANEL):
             r = 1.0 / cols[k][k : k + 1, :]
-            f = jnp.where(rw > p0 + k, cols[k] * r, 0.0)
+            below = jnp.where(rw > p0 + k, cols[k], 0.0)
             for j in range(k + 1, PANEL):
-                cols[j] = cols[j] - f * cols[j][k : k + 1, :]
-            pivot_row = jnp.where(ln[0:1] == p0 + k, 1.0, low[k : k + 1, :])
+                cols[j] = cols[j] - below * (cols[j][k : k + 1, :] * r)
+            pivot_row = jnp.where(ln[0:1] == p0 + k, 1.0, low[k : k + 1, :]) * r
             cleared = jnp.where((ln == p0 + k) & (rw > p0 + k), 0.0, low)
-            low = cleared - f * pivot_row
+            low = cleared - below * pivot_row
         block = jnp.concatenate([block[:p0], low], axis=0) if p0 else low
         service()
     return block
@@ -299,24 +299,23 @@
     )
     start_ag1(1)
     start_rs2(4)
+    start_ag1(2)
     start_ag1(0)
-    start_ag1(2)
     g3.wait_recv()
     ours = gsum.at[:, c]
     g4 = send([(ours, ours, other)], both(g_s, g_r, 3), ours)
     start_ag1(3)
     start_ag2(1)
-    start_ag2(0)
-    start_ag1(4)
     g4.wait_recv()
     for i in range(NX):
         for k in range(2):
             gmat[64 * i + 32 * k : 64 * i + 32 * k + 32, :] = gsum[i, k]
 
     plan = {
+        0: [(start_ag1, 4), (start_ag2, 0)],
         2: [(start_ag2, 2)],
-        5: [(start_ag2, 3)],
-        9: [(start_ag2, 4)],
+        4: [(start_ag2, 3)],
+        7: [(start_ag2, 4)],
     }
     panels = []
 
@@ -331,13 +330,16 @@
     inv = split(jnp.where(row >= lane, gmat[...], 0.0))
     q = dot3(split(pfull[0]), (inv[0][:, :HALF], inv[1][:, :HALF]), 1, 1)
     q = q + dot3(split(pfull[1]), (inv[0][:, HALF:], inv[1][:, HALF:]), 1, 1)
-    for n in range(len(CHUNKS)):
-        ag2[n].wait_recv()
-    rt = dot3(inv, split(wf[...]), 1, 0)
-    squares = rt[:, :128] * rt[:, :128]
-    for k in range(1, BC // 128):
-        piece = rt[:, k * 128 : (k + 1) * 128]
-        squares = squares + piece * piece
+    parts, squares = {}, 0.0
+    for ns in ((0, 1, 2), (3,), (4,)):
+        for n in ns:
+            ag2[n].wait_recv()
+        c0, c1 = CHUNKS[ns[0]][0], CHUNKS[ns[-1]][0] + CHUNKS[ns[-1]][1]
+        parts[c0] = dot3(inv, split(wf[:, c0:c1]), 1, 0)
+        for k in range(0, c1 - c0, 128):
+            piece = parts[c0][:, k : k + 128]
+            squares = squares + piece * piece
+    rt = jnp.concatenate([parts[c0] for c0 in sorted(parts)], axis=1)
     squares = squares.T
     total = squares[0:8, :]
     for k in range(1, 16):

time: 66.3 us -> 63 us (0.950)
  Pallas kernels: 65.6 us -> 62.3 us
    pallas_call x1, Pallas kernels: 62.9 us -> 59.6 us  [body(): pl.pallas_call(factor_kernel, out_shape=inner, in_specs=[pl.BlockSpec(mem...]
where the time goes in v4:
time: 63 us; the launch traced here: 62.9 us
  Pallas kernels  62.3 us (99%)
  between operations  0.64 us (1%)
    pallas_call x1, Pallas kernels, body(): pl.pallas_call(factor_kernel, out_shape=inner, in_specs=[pl.BlockSpec(mem...  59.6 us
    pallas_call x1, Pallas kernels, body(): pl.pallas_call(output_kernel, out_shape=(jax.ShapeDtypeStruct((BR, BC), F...  2.67 us

profile of v4, /device:TPU:1, one launch (start us, length us, event | category | flops | bytes accessed | tf_op | source)
XLA Modules:
  0.0 62.9 jit_solution(7345353405694185492)
XLA Ops:
  0.6 59.6 %factors.1 = (f32[512,1152]{1,0:T(8,128)S(1)}, f32[512,1152]{1,0:T(8,128)S(1)}, f32[512,256]{1,0:T(8,128)S(1)}, bf16[256,1152]{1,0:T(8,128)(2,1)S(1)}, bf16[256,...) custom-call(f32[512,1152]{1,0:T(8,128)} %m_ref.1, bf16[512,1152]{1,0:T(8,128)(2,1)} %g_ref.1, ...), custom_call_target="tpu_custom_call" | custom-call | tf_op jit(solution)/shard_map/factors/pallas_call | solution.py:401
  60.3 2.7 %outputs.1 = (f32[512,1152]{1,0:T(8,128)}, f32[512,1152]{1,0:T(8,128)}, f32[1152,256]{1,0:T(8,128)}) custom-call(f32[512,1152]{1,0:T(8,128)S(1)} %get-tuple-element.10.nm_ref, f32[512,1152]{1,0:T(8,128)S(1)} %get-tuple-element.11.wv_ref, f32[512,256]{1,0:T(8,128)S(1)} %get-tuple-element.12.q_ref, bf16[256,1152]{1,0:T(8,128)(2,1)S(1)} %get-tuple-element.13.rh_ref, ...), custom_call_target="tpu_custom_call" | custom-call | tf_op jit(solution)/shard_map/outputs/pallas_call | solution.py:446

commit v5 on v4

--- a/solution.py
+++ b/solution.py
@@ -328,8 +328,6 @@
     row = lax.broadcasted_iota(jnp.int32, (RANK, RANK), 0)
     lane = lax.broadcasted_iota(jnp.int32, (RANK, RANK), 1)
     inv = split(jnp.where(row >= lane, gmat[...], 0.0))
-    q = dot3(split(pfull[0]), (inv[0][:, :HALF], inv[1][:, :HALF]), 1, 1)
-    q = q + dot3(split(pfull[1]), (inv[0][:, HALF:], inv[1][:, HALF:]), 1, 1)
     parts, squares = {}, 0.0
     for ns in ((0, 1, 2), (3,), (4,)):
         for n in ns:
@@ -346,6 +344,8 @@
         total = total + squares[8 * k : 8 * k + 8, :]
     nbuf[ti] = total
     n1 = send([(nbuf.at[ti], nbuf.at[ti], p) for p in tensor_peers], both(n_s, n_r, 0), nbuf.at[pl.ds(0, 2 * NX - 1)])
+    q = dot3(split(pfull[0]), (inv[0][:, :HALF], inv[1][:, :HALF]), 1, 1)
+    q = q + dot3(split(pfull[1]), (inv[0][:, HALF:], inv[1][:, HALF:]), 1, 1)
     rsplit = split(rt)
     rh_ref[...], rl_ref[...] = rsplit
     for k in range(2):
@@ -353,6 +353,9 @@
         qk = jnp.where(c == k, q[256:], q[:256])
         nm_ref[rows, :] = mv[k] + gv[k].astype(F32) - dot3(split(0.5 * qk), rsplit, 1, 0)
     rtt_ref[...] = rt.T
+    load_w.wait()
+    for cp in pending[:-1]:
+        cp.wait_send()
     n1.wait_recv()
     total = nbuf[0]
     for i in range(1, 2 * NX):
@@ -361,9 +364,7 @@
     scale = lax.rsqrt(total / COLS + 1e-06)
     norm_ref[...] = jnp.broadcast_to(scale, (8, RANK))
     q_ref[...] = q * (scale * (0.2 * math.sqrt(ROWS / RANK)))
-    load_w.wait()
-    for cp in pending:
-        cp.wait_send()
+    n1.wait_send()
 
 
 def output_kernel(nm_ref, wv_ref, q_ref, rh_ref, rl_ref, rtt_ref, norm_ref, onm_ref, onw_ref, onr_ref, nw, nr, sems):

time: 63 us -> 62.7 us (level)
  no operation moved by 1% of the time
where the time goes in v5:
time: 62.7 us; the launch traced here: 62.6 us
  Pallas kernels  62 us (99%)
  between operations  0.64 us (1%)
    pallas_call x1, Pallas kernels, body(): pl.pallas_call(factor_kernel, out_shape=inner, in_specs=[pl.BlockSpec(mem...  59.3 us
    pallas_call x1, Pallas kernels, body(): pl.pallas_call(output_kernel, out_shape=(jax.ShapeDtypeStruct((BR, BC), F...  2.67 us

profile of v5, /device:TPU:1, one launch (start us, length us, event | category | flops | bytes accessed | tf_op | source)
XLA Modules:
  0.0 62.6 jit_solution(7916668536862726056)
XLA Ops:
  0.6 59.3 %factors.1 = (f32[512,1152]{1,0:T(8,128)S(1)}, f32[512,1152]{1,0:T(8,128)S(1)}, f32[512,256]{1,0:T(8,128)S(1)}, bf16[256,1152]{1,0:T(8,128)(2,1)S(1)}, bf16[256,...) custom-call(f32[512,1152]{1,0:T(8,128)} %m_ref.1, bf16[512,1152]{1,0:T(8,128)(2,1)} %g_ref.1, ...), custom_call_target="tpu_custom_call" | custom-call | tf_op jit(solution)/shard_map/factors/pallas_call | solution.py:402
  59.9 2.7 %outputs.1 = (f32[512,1152]{1,0:T(8,128)}, f32[512,1152]{1,0:T(8,128)}, f32[1152,256]{1,0:T(8,128)}) custom-call(f32[512,1152]{1,0:T(8,128)S(1)} %get-tuple-element.10.nm_ref, f32[512,1152]{1,0:T(8,128)S(1)} %get-tuple-element.11.wv_ref, f32[512,256]{1,0:T(8,128)S(1)} %get-tuple-element.12.q_ref, bf16[256,1152]{1,0:T(8,128)(2,1)S(1)} %get-tuple-element.13.rh_ref, ...), custom_call_target="tpu_custom_call" | custom-call | tf_op jit(solution)/shard_map/outputs/pallas_call | solution.py:447

commit v6 on v5

--- a/solution.py
+++ b/solution.py
@@ -196,12 +196,12 @@
         if h == 0:
             w[:HALF, :] = dot3(split(ph), (bh[...], bl[...]), 1, 0)
 
-    rows = ds(32 * ti, 32)
+    rows = ds(64 * x, 64)
     ptr = pt[rows, :]
     for h in range(2):
         gpart[:, h * HALF : (h + 1) * HALF] = dot_f32(ptr, pfull[h], 1, 0)
     g1 = send(
-        [(gpart.at[ds(8 * peer_y(i), 8)], gyrecv.at[i - 1], dev(z, peer_y(i), x, c)) for i in range(1, NY)],
+        [(gpart.at[ds(16 * peer_y(i), 16)], gyrecv.at[i - 1], dev(z, peer_y(i), x, c)) for i in range(1, NY)],
         both(g_s, g_r, 0), gyrecv,
     )
     w[HALF:, :] = dot3(split(ph), (bh[...], bl[...]), 1, 0)
@@ -278,7 +278,7 @@
     for n in range(len(CHUNKS)):
         start_rs1(n)
     g1.wait_recv()
-    total = gpart[ds(8 * y, 8), :]
+    total = gpart[ds(16 * y, 16), :]
     for i in range(NY - 1):
         total = total + gyrecv[i]
     gz[z] = total
@@ -291,25 +291,21 @@
     total = gz[0]
     for i in range(1, NZ):
         total = total + gz[i]
-    mine = gsum.at[x, c, ds(8 * y, 8)]
+    mine = gsum.at[x, ds(16 * y, 16)]
     mine[...] = total
     g3 = send(
         [(mine, mine, dev(z, peer_y(j), peer_x(i), c)) for i in range(NX) for j in range(NY) if i or j],
-        both(g_s, g_r, 2), w.at[pl.ds(0, 8 * (NX * NY - 1)), pl.ds(0, RANK)],
+        both(g_s, g_r, 2), w.at[pl.ds(0, 16 * (NX * NY - 1)), pl.ds(0, RANK)],
     )
     start_ag1(1)
     start_rs2(4)
     start_ag1(2)
     start_ag1(0)
     g3.wait_recv()
-    ours = gsum.at[:, c]
-    g4 = send([(ours, ours, other)], both(g_s, g_r, 3), ours)
     start_ag1(3)
     start_ag2(1)
-    g4.wait_recv()
     for i in range(NX):
-        for k in range(2):
-            gmat[64 * i + 32 * k : 64 * i + 32 * k + 32, :] = gsum[i, k]
+        gmat[64 * i : 64 * i + 64, :] = gsum[i]
 
     plan = {
         0: [(start_ag1, 4), (start_ag2, 0)],
@@ -417,10 +413,10 @@
             pltpu.VMEM((2, 64, HALF), F32),
             pltpu.VMEM((2, BR, HALF), F32),
             pltpu.VMEM((RANK, BR), F32),
-            pltpu.VMEM((32, RANK), F32),
-            pltpu.VMEM((NY - 1, 8, RANK), F32),
-            pltpu.VMEM((NZ, 8, RANK), F32),
-            pltpu.VMEM((NX, 2, 32, RANK), F32),
+            pltpu.VMEM((64, RANK), F32),
+            pltpu.VMEM((NY - 1, 16, RANK), F32),
+            pltpu.VMEM((NZ, 16, RANK), F32),
+            pltpu.VMEM((NX, 64, RANK), F32),
             pltpu.VMEM((RANK, RANK), F32),
             pltpu.VMEM((RANK, BC), F32),
             pltpu.VMEM((RANK, BC), F32),
@@ -435,7 +431,7 @@
             dma((6,)),
             dma((2, 2)), dma((2, 2)),
             dma((2, 2)), dma((2, 2)),
-            dma((4,)), dma((4,)),
+            dma((3,)), dma((3,)),
             dma((len(CHUNKS), 4)), dma((len(CHUNKS), 4)),
             dma((1,)), dma((1,)),
         ],

time: 62.7 us -> 64 us (1.021)
  Pallas kernels: 62 us -> 63.3 us
    pallas_call x1, Pallas kernels: 59.3 us -> 60.6 us  [body(): pl.pallas_call(factor_kernel, out_shape=inner, in_specs=[pl.BlockSpec(mem...]
where the time goes in v6:
time: 64 us; the launch traced here: 63.9 us
  Pallas kernels  63.3 us (99%)
  between operations  0.64 us (1%)
    pallas_call x1, Pallas kernels, body(): pl.pallas_call(factor_kernel, out_shape=inner, in_specs=[pl.BlockSpec(mem...  60.6 us
    pallas_call x1, Pallas kernels, body(): pl.pallas_call(output_kernel, out_shape=(jax.ShapeDtypeStruct((BR, BC), F...  2.67 us

profile of v6, /device:TPU:1, one launch (start us, length us, event | category | flops | bytes accessed | tf_op | source)
XLA Modules:
  0.0 63.9 jit_solution(4362491099280118963)
XLA Ops:
  0.6 60.6 %factors.1 = (f32[512,1152]{1,0:T(8,128)S(1)}, f32[512,1152]{1,0:T(8,128)S(1)}, f32[512,256]{1,0:T(8,128)S(1)}, bf16[256,1152]{1,0:T(8,128)(2,1)S(1)}, bf16[256,...) custom-call(f32[512,1152]{1,0:T(8,128)} %m_ref.1, bf16[512,1152]{1,0:T(8,128)(2,1)} %g_ref.1, ...), custom_call_target="tpu_custom_call" | custom-call | tf_op jit(solution)/shard_map/factors/pallas_call | solution.py:398
  61.2 2.7 %outputs.1 = (f32[512,1152]{1,0:T(8,128)}, f32[512,1152]{1,0:T(8,128)}, f32[1152,256]{1,0:T(8,128)}) custom-call(f32[512,1152]{1,0:T(8,128)S(1)} %get-tuple-element.10.nm_ref, f32[512,1152]{1,0:T(8,128)S(1)} %get-tuple-element.11.wv_ref, f32[512,256]{1,0:T(8,128)S(1)} %get-tuple-element.12.q_ref, bf16[256,1152]{1,0:T(8,128)(2,1)S(1)} %get-tuple-element.13.rh_ref, ...), custom_call_target="tpu_custom_call" | custom-call | tf_op jit(solution)/shard_map/outputs/pallas_call | solution.py:443
